TPU v7x, 32 devices: a whole 2x2x4 slice. The times are simulated.
32 devices in a mesh: ctx: 8 (over y, x, core), tp: 4 (over z).
Axes of the slice: x: 2, y: 2, z: 4, core: 2. Of those that a mesh axis runs over, the one named last changes fastest.
Arguments:
- tokens: bfloat16 [4096, 4096], P('ctx'), may hold values from -6 to 6
- query_weight: bfloat16 [4096, 512], P(None, 'tp'), may hold values from -0.09375 to 0.09375
- key_weight: bfloat16 [4096, 512], P(None, 'tp'), may hold values from -0.09375 to 0.09375
- value_weight: bfloat16 [4096, 4096], P(None, 'tp'), may hold values from -0.09375 to 0.09375
- norm_gain: bfloat16 [4096], P('tp'), may hold values from 0.5 to 1.5
- out_weight: bfloat16 [4096, 4096], P('tp'), may hold values from -0.09375 to 0.09375
Outputs:
- attended: bfloat16 [4096, 4096], P('ctx', 'tp')
All inputs are finite; a program needn't handle non-finite values.
Results may differ from a plain program's by a relative error of at most 0.03.
Values may be sent and summed in bfloat16 or wider, within the bound.
No kernel may reach another device: no remote copies, remote signals or barrier semaphores. Data moves between devices by JAX's collectives and lax.ppermute only.
A program may use at most 128 MiB of HBM per device.

v0:
```python
import jax
import jax.numpy as jnp
from jax import lax
from jax.sharding import PartitionSpec as P

F = 16
DV = 128


half_root = 0.7071067811865476


def passed_along(block, axis, distance):
    devices = range(lax.axis_size(axis))
    route = [(i - distance, i) for i in devices if i - distance in devices]
    return lax.ppermute(block, axis, route)


def project(inputs, weight, factor):
    return (jnp.dot(inputs, weight, preferred_element_type=jnp.float32) * factor).astype(
        jnp.bfloat16
    )


def pairs_of(features):
    rows, heads, width = features.shape
    wide = features.astype(jnp.float32)
    outer = wide[:, :, :, None] * wide[:, :, None, :] * half_root
    return outer.reshape(rows, heads, width * width).astype(jnp.bfloat16)


def add_states(earlier, later):
    return jax.tree.map(jnp.add, earlier, later)


def per_device(tokens, query_weight, key_weight, value_weight, norm_gain, out_weight):
    highest = lax.Precision.HIGHEST
    rows = tokens.shape[0]
    heads = norm_gain.shape[0] // DV
    factor = F ** (-0.25)
    query_rows = project(tokens, query_weight, factor).reshape(rows, heads, F)
    key_rows = project(tokens, key_weight, factor).reshape(rows, heads, F)
    value_rows = project(tokens, value_weight, 1.0).reshape(rows, heads, DV)
    query_pairs = pairs_of(query_rows)
    key_pairs = pairs_of(key_rows)
    local_states = (
        jnp.einsum("thp,thd->hpd", key_pairs, value_rows, preferred_element_type=jnp.float32),
        jnp.einsum("thf,thd->hfd", key_rows, value_rows, preferred_element_type=jnp.float32),
        jnp.sum(value_rows.astype(jnp.float32), axis=0),
        jnp.sum(key_pairs.astype(jnp.float32), axis=0),
        jnp.sum(key_rows.astype(jnp.float32), axis=0),
    )
    empty_states = jax.tree.map(jnp.zeros_like, local_states)

    def relay(turn_index, carried):
        summed = add_states(carried, local_states)
        return (
            passed_along(summed[0].astype(jnp.bfloat16), "ctx", 1).astype(jnp.float32),
            passed_along(summed[1].astype(jnp.bfloat16), "ctx", 1).astype(jnp.float32),
            passed_along(summed[2].astype(jnp.bfloat16), "ctx", 1).astype(jnp.float32),
            passed_along(summed[3].astype(jnp.bfloat16), "ctx", 1).astype(jnp.float32),
            passed_along(summed[4].astype(jnp.bfloat16), "ctx", 1).astype(jnp.float32),
        )

    prefix_states = lax.fori_loop(0, lax.axis_size("ctx") - 1, relay, empty_states)
    prev_pairs, prev_linear, prev_values, prev_pair_sums, prev_key_sums = prefix_states
    scores = jnp.einsum("thf,shf->hts", query_rows, key_rows, preferred_element_type=jnp.float32)
    causal_mask = jnp.tril(jnp.ones((rows, rows), jnp.float32)) > 0.5
    local_weights = jnp.where(causal_mask[None], 1.0 + scores + 0.5 * scores * scores, 0.0)
    rounded_weights = local_weights.astype(jnp.bfloat16)
    local_numerator = jnp.einsum(
        "hts,shd->thd", rounded_weights, value_rows, preferred_element_type=jnp.float32
    )
    local_denominator = jnp.transpose(jnp.sum(local_weights, axis=2))
    query_wide = query_rows.astype(jnp.float32)
    qpair_wide = query_pairs.astype(jnp.float32)
    numerator = prev_values[None] + jnp.einsum(
        "thf,hfd->thd", query_wide, prev_linear, precision=highest
    )
    numerator = numerator + jnp.einsum("thp,hpd->thd", qpair_wide, prev_pairs, precision=highest)
    numerator = numerator + local_numerator
    offset_count = lax.axis_index("ctx").astype(jnp.float32) * rows
    denominator = offset_count + jnp.einsum(
        "thf,hf->th", query_wide, prev_key_sums, precision=highest
    )
    denominator = denominator + jnp.einsum(
        "thp,hp->th", qpair_wide, prev_pair_sums, precision=highest
    )
    denominator = denominator + local_denominator
    ratio = numerator / denominator[:, :, None]
    spread = jnp.mean(ratio * ratio, axis=2, keepdims=True)
    gain_heads = norm_gain.astype(jnp.float32).reshape(heads, DV)
    normalized = (ratio / jnp.sqrt(spread + 1e-06) * gain_heads[None]).astype(jnp.bfloat16)
    normalized = normalized.reshape(rows, heads * DV)
    partial_value = jnp.dot(normalized, out_weight, preferred_element_type=jnp.float32)
    return lax.psum_scatter(
        partial_value.astype(jnp.bfloat16), "tp", scatter_dimension=1, tiled=True
    )


def solution(mesh):
    in_specs = (P("ctx", None), P(None, "tp"), P(None, "tp"), P(None, "tp"), P("tp"), P("tp", None))
    out_specs = P("ctx", "tp")
    return jax.shard_map(
        per_device, mesh=mesh, in_specs=in_specs, out_specs=out_specs, check_vma=False
    )
```

profile of v0, /device:TPU:0, one launch (start us, length us, event | category | flops | bytes accessed | tf_op | source)
XLA Modules:
  0.0 271.7 jit_solution(5072517111236044073)
XLA Ops:
  8.8 4.0 %fusion.17 = bf16[512,128]{0,1:T(8,128)(2,1)S(1)} fusion(bf16[512,4096]{1,0:T(8,128)(2,1)} %param.8, bf16[4096,128]{1,0:T(8,128)(2,1)} %param.9), kind=kOutput, calls=%fused_computation.33 | convolution fusion | flops 537001984 | bytes 5373952 | tf_op jit(solution)/shard_map/dot_general | solution.py:20
  15.9 10.7 %convert_reduce_fusion.1 = (f32[1024]{0:T(1024)}, bf16[512,1024]{1,0:T(8,128)(2,1)}) fusion(bf16[512,4096]{1,0:T(8,128)(2,1)} %param.8, bf16[4096,1024]{1,0:T(8,128)(2,1)} %param.11), kind=kOutput, calls=%fused_computation.27 | convolution fusion | flops 4296539136 | bytes 13635584 | tf_op jit(solution)/shard_map/dot_general | solution.py:20
  28.1 3.4 %multiply_convert_fusion = bf16[512,8,16,16]{0,3,2,1:T(8,128)(2,1)} fusion(f32[512,8,16]{0,2,1:T(8,128)} %bitcast_convert_fusion.2), kind=kLoop, calls=%fused_computation.16 | loop fusion | flops 3145728 | bytes 2359296 | tf_op jit(solution)/shard_map/convert_element_type | solution.py:29
  37.3 123.7 %while.19 = (s32[]{:T(128)}, f32[8,256,128]{2,1,0:T(8,128)S(1)}, f32[8,16,128]{2,1,0:T(8,128)S(1)}, f32[8,128]{1,0:T(8,128)}, f32[8,256]{1,0:T(8,128)S(1)}, /*in...) while((s32[]{:T(128)}, f32[8,256,128]{2,1,0:T(8,128)S(1)}, ...), condition=%wide.region_4.0_spmd.clone, body=%wide.region_3.0_spmd.clone.sunk | while | flops 1126915 | bytes 6761811 | solution.py:65
  41.3 5.3 %collective-permute-start = (bf16[8,256,128]{2,1,0:T(8,128)(2,1)}, bf16[8,256,128]{2,1,0:T(8,128)(2,1)}, u32[]{:S(2)}, u32[]{:S(2)}) collective-permute-start(bf16[8,256,128]{2,1,0:T(8,128)(2,1)} %fusion.56), channel_id=1, source_target_pairs={{0,4},{4,8},{8,12},{12,16},{16,20},{20,24},{24,28},{1,5},{5,9},{9,... | collective-permute-start | bytes 1572872 | tf_op jit(solution)/shard_map/while/body/eval_jaxpr/ppermute | solution.py:16
  47.9 3.3 %collective-permute-start.1 = (bf16[8,16,128]{2,1,0:T(8,128)(2,1)S(1)}, bf16[8,16,128]{2,1,0:T(8,128)(2,1)S(1)}, u32[]{:S(2)}, u32[]{:S(2)}) collective-permute-start(bf16[8,16,128]{2,1,0:T(8,128)(2,1)S(1)} %fusion.57), channel_id=1, source_target_pairs={{0,4},{4,8},{8,12},{12,16},{16,20},{20,24},{24,28},{1,5},{5,9},{9,... | collective-permute-start | bytes 98312 | tf_op jit(solution)/shard_map/while/body/eval_jaxpr/ppermute | solution.py:16
  56.5 3.4 %collective-permute-start.2 = (bf16[8,128]{1,0:T(8,128)(2,1)S(1)}, bf16[8,128]{1,0:T(8,128)(2,1)S(1)}, u32[]{:S(2)}, u32[]{:S(2)}) collective-permute-start(bf16[8,128]{1,0:T(8,128)(2,1)S(1)} %fusion.58), channel_id=1, source_target_pairs={{0,4},{4,8},{8,12},{12,16},{16,20},{20,24},{24,28},{1,5},{5,9},{9,... | collective-permute-start | bytes 6152 | tf_op jit(solution)/shard_map/while/body/eval_jaxpr/ppermute | solution.py:16
  60.8 5.0 %collective-permute-start = (bf16[8,256,128]{2,1,0:T(8,128)(2,1)}, bf16[8,256,128]{2,1,0:T(8,128)(2,1)}, u32[]{:S(2)}, u32[]{:S(2)}) collective-permute-start(bf16[8,256,128]{2,1,0:T(8,128)(2,1)} %fusion.56), channel_id=1, source_target_pairs={{0,4},{4,8},{8,12},{12,16},{16,20},{20,24},{24,28},{1,5},{5,9},{9,... | collective-permute-start | bytes 1572872 | tf_op jit(solution)/shard_map/while/body/eval_jaxpr/ppermute | solution.py:16
  67.1 2.7 collective-permute-start.1
  78.1 4.6 %collective-permute-start = (bf16[8,256,128]{2,1,0:T(8,128)(2,1)}, bf16[8,256,128]{2,1,0:T(8,128)(2,1)}, u32[]{:S(2)}, u32[]{:S(2)}) collective-permute-start(bf16[8,256,128]{2,1,0:T(8,128)(2,1)} %fusion.56), channel_id=1, source_target_pairs={{0,4},{4,8},{8,12},{12,16},{16,20},{20,24},{24,28},{1,5},{5,9},{9,... | collective-permute-start | bytes 1572872 | tf_op jit(solution)/shard_map/while/body/eval_jaxpr/ppermute | solution.py:16
  84.0 3.1 %collective-permute-start.1 = (bf16[8,16,128]{2,1,0:T(8,128)(2,1)S(1)}, bf16[8,16,128]{2,1,0:T(8,128)(2,1)S(1)}, u32[]{:S(2)}, u32[]{:S(2)}) collective-permute-start(bf16[8,16,128]{2,1,0:T(8,128)(2,1)S(1)} %fusion.57), channel_id=1, source_target_pairs={{0,4},{4,8},{8,12},{12,16},{16,20},{20,24},{24,28},{1,5},{5,9},{9,... | collective-permute-start | bytes 98312 | tf_op jit(solution)/shard_map/while/body/eval_jaxpr/ppermute | solution.py:16
  95.5 4.6 %collective-permute-start = (bf16[8,256,128]{2,1,0:T(8,128)(2,1)}, bf16[8,256,128]{2,1,0:T(8,128)(2,1)}, u32[]{:S(2)}, u32[]{:S(2)}) collective-permute-start(bf16[8,256,128]{2,1,0:T(8,128)(2,1)} %fusion.56), channel_id=1, source_target_pairs={{0,4},{4,8},{8,12},{12,16},{16,20},{20,24},{24,28},{1,5},{5,9},{9,... | collective-permute-start | bytes 1572872 | tf_op jit(solution)/shard_map/while/body/eval_jaxpr/ppermute | solution.py:16
  101.4 3.1 %collective-permute-start.1 = (bf16[8,16,128]{2,1,0:T(8,128)(2,1)S(1)}, bf16[8,16,128]{2,1,0:T(8,128)(2,1)S(1)}, u32[]{:S(2)}, u32[]{:S(2)}) collective-permute-start(bf16[8,16,128]{2,1,0:T(8,128)(2,1)S(1)} %fusion.57), channel_id=1, source_target_pairs={{0,4},{4,8},{8,12},{12,16},{16,20},{20,24},{24,28},{1,5},{5,9},{9,... | collective-permute-start | bytes 98312 | tf_op jit(solution)/shard_map/while/body/eval_jaxpr/ppermute | solution.py:16
  112.8 4.6 %collective-permute-start = (bf16[8,256,128]{2,1,0:T(8,128)(2,1)}, bf16[8,256,128]{2,1,0:T(8,128)(2,1)}, u32[]{:S(2)}, u32[]{:S(2)}) collective-permute-start(bf16[8,256,128]{2,1,0:T(8,128)(2,1)} %fusion.56), channel_id=1, source_target_pairs={{0,4},{4,8},{8,12},{12,16},{16,20},{20,24},{24,28},{1,5},{5,9},{9,... | collective-permute-start | bytes 1572872 | tf_op jit(solution)/shard_map/while/body/eval_jaxpr/ppermute | solution.py:16
  118.7 3.1 %collective-permute-start.1 = (bf16[8,16,128]{2,1,0:T(8,128)(2,1)S(1)}, bf16[8,16,128]{2,1,0:T(8,128)(2,1)S(1)}, u32[]{:S(2)}, u32[]{:S(2)}) collective-permute-start(bf16[8,16,128]{2,1,0:T(8,128)(2,1)S(1)} %fusion.57), channel_id=1, source_target_pairs={{0,4},{4,8},{8,12},{12,16},{16,20},{20,24},{24,28},{1,5},{5,9},{9,... | collective-permute-start | bytes 98312 | tf_op jit(solution)/shard_map/while/body/eval_jaxpr/ppermute | solution.py:16
  130.2 4.6 %collective-permute-start = (bf16[8,256,128]{2,1,0:T(8,128)(2,1)}, bf16[8,256,128]{2,1,0:T(8,128)(2,1)}, u32[]{:S(2)}, u32[]{:S(2)}) collective-permute-start(bf16[8,256,128]{2,1,0:T(8,128)(2,1)} %fusion.56), channel_id=1, source_target_pairs={{0,4},{4,8},{8,12},{12,16},{16,20},{20,24},{24,28},{1,5},{5,9},{9,... | collective-permute-start | bytes 1572872 | tf_op jit(solution)/shard_map/while/body/eval_jaxpr/ppermute | solution.py:16
  136.0 3.1 %collective-permute-start.1 = (bf16[8,16,128]{2,1,0:T(8,128)(2,1)S(1)}, bf16[8,16,128]{2,1,0:T(8,128)(2,1)S(1)}, u32[]{:S(2)}, u32[]{:S(2)}) collective-permute-start(bf16[8,16,128]{2,1,0:T(8,128)(2,1)S(1)} %fusion.57), channel_id=1, source_target_pairs={{0,4},{4,8},{8,12},{12,16},{16,20},{20,24},{24,28},{1,5},{5,9},{9,... | collective-permute-start | bytes 98312 | tf_op jit(solution)/shard_map/while/body/eval_jaxpr/ppermute | solution.py:16
  147.5 4.6 %collective-permute-start = (bf16[8,256,128]{2,1,0:T(8,128)(2,1)}, bf16[8,256,128]{2,1,0:T(8,128)(2,1)}, u32[]{:S(2)}, u32[]{:S(2)}) collective-permute-start(bf16[8,256,128]{2,1,0:T(8,128)(2,1)} %fusion.56), channel_id=1, source_target_pairs={{0,4},{4,8},{8,12},{12,16},{16,20},{20,24},{24,28},{1,5},{5,9},{9,... | collective-permute-start | bytes 1572872 | tf_op jit(solution)/shard_map/while/body/eval_jaxpr/ppermute | solution.py:16
  153.4 3.1 %collective-permute-start.1 = (bf16[8,16,128]{2,1,0:T(8,128)(2,1)S(1)}, bf16[8,16,128]{2,1,0:T(8,128)(2,1)S(1)}, u32[]{:S(2)}, u32[]{:S(2)}) collective-permute-start(bf16[8,16,128]{2,1,0:T(8,128)(2,1)S(1)} %fusion.57), channel_id=1, source_target_pairs={{0,4},{4,8},{8,12},{12,16},{16,20},{20,24},{24,28},{1,5},{5,9},{9,... | collective-permute-start | bytes 98312 | tf_op jit(solution)/shard_map/while/body/eval_jaxpr/ppermute | solution.py:16
  163.5 4.1 %fusion.27 = f32[8,128,512]{2,1,0:T(8,128)} fusion(f32[8,256,128]{2,1,0:T(8,128)S(1)} %get-tuple-element.68, bf16[512,8,256]{0,2,1:T(8,128)(2,1)} %bitcast.62), kind=kOutput, calls=%fused_computation.52 | convolution fusion | flops 1610612736 | bytes 5242880 | tf_op jit(solution)/shard_map/thp,hpd->thd/dot_general | solution.py:80
  170.4 3.1 %fusion.9 = f32[8,128,512]{2,1,0:T(8,128)} fusion(bf16[512,8,128]{0,2,1:T(8,128)(2,1)S(1)} %bitcast.65, f32[8,512,512]{1,2,0:T(8,128)S(1)} %get-tuple-element.136, pred[512,512]{0,1:T(8,128)(4,1)S(1)} %copy-done.8), kind=kOutput, calls=%fused_computation.19 | convolution fusion | flops 549453824 | bytes 11796480 | tf_op jit(solution)/shard_map/hts,shd->thd/dot_general | solution.py:71
  173.5 3.7 %fusion.15 = (f32[512,8]{0,1:T(8,128)S(1)}, f32[8,128,512]{2,1,0:T(8,128)S(1)}) fusion(f32[512,8]{0,1:T(8,128)S(1)} %fusion.19, f32[8,128,512]{2,1,0:T(8,128)} %fusion.9, f32[8,128,512]{2,1,0:T(8,128)} %fusion.27, f32[8,16,128]{2,1,0:T(8,128)S(1)} %get-tuple-element.67, bf16[512,8,16]{0,2,1:T(8,128)(2,1)S(1)} %bitcast.69, f32[8,128]{1,0:T(8,128)S(1)} %copy-done.9), kind=kOutput, calls=%fused_computation.28 | convolution fusion | flops 103804928 | bytes 6524928 | tf_op jit(solution)/shard_map/thf,hfd->thd/dot_general | solution.py:77
  177.5 9.5 %convolution_convert_fusion = bf16[512,4096]{1,0:T(8,128)(2,1)} fusion(bf16[512,1024]{0,1:T(8,128)(2,1)S(1)} %bitcast.72, bf16[1024,4096]{1,0:T(8,128)(2,1)} %param.13), kind=kOutput, calls=%fused_computation.13 | convolution fusion | flops 4297064448 | bytes 13631488 | tf_op jit(solution)/shard_map/dot_general | solution.py:95
  187.0 77.8 %reduce-scatter.2.cloned.1.call-done = bf16[512,1024]{1,0:T(8,128)(2,1)} async-done(((bf16[512,4096]{1,0:T(8,128)(2,1)}), bf16[512,1024]{1,0:T(8,128)(2,1)}) %reduce-scatter.2.cloned.1.call-update) | async-done | bytes 1048592 | tf_op jit(solution)/shard_map/reduce_scatter | solution.py:96
  (171 shorter events, 83.3 us)
Async XLA Ops:
  6.5 258.3 %reduce-scatter.2.cloned.1.call-start = ((), (), s32[]{:S(2)}) async-start(), calls=%async_computation.1 | async-start | bytes 5242880 | tf_op jit(solution)/shard_map/reduce_scatter | solution.py:96
  38.0 16.0 %collective-permute-start.2 = (bf16[8,128]{1,0:T(8,128)(2,1)S(1)}, bf16[8,128]{1,0:T(8,128)(2,1)S(1)}, u32[]{:S(2)}, u32[]{:S(2)}) collective-permute-start(bf16[8,128]{1,0:T(8,128)(2,1)S(1)} %fusion.58), channel_id=1, source_target_pairs={{0,4},{4,8},{8,12},{12,16},{16,20},{20,24},{24,28},{1,5},{5,9},{9,... | collective-permute-start | bytes 6152 | tf_op jit(solution)/shard_map/while/body/eval_jaxpr/ppermute | solution.py:16
  41.3 13.4 %collective-permute-start = (bf16[8,256,128]{2,1,0:T(8,128)(2,1)}, bf16[8,256,128]{2,1,0:T(8,128)(2,1)}, u32[]{:S(2)}, u32[]{:S(2)}) collective-permute-start(bf16[8,256,128]{2,1,0:T(8,128)(2,1)} %fusion.56), channel_id=1, source_target_pairs={{0,4},{4,8},{8,12},{12,16},{16,20},{20,24},{24,28},{1,5},{5,9},{9,... | collective-permute-start | bytes 1572872 | tf_op jit(solution)/shard_map/while/body/eval_jaxpr/ppermute | solution.py:16
  46.6 8.0 %collective-permute-start.3 = (bf16[8,256]{1,0:T(8,128)(2,1)S(1)}, bf16[8,256]{1,0:T(8,128)(2,1)S(1)}, u32[]{:S(2)}, u32[]{:S(2)}) collective-permute-start(bf16[8,256]{1,0:T(8,128)(2,1)S(1)} %fusion.59), channel_id=1, source_target_pairs={{0,4},{4,8},{8,12},{12,16},{16,20},{20,24},{24,28},{1,5},{5,9},{9,... | collective-permute-start | bytes 12296 | tf_op jit(solution)/shard_map/while/body/eval_jaxpr/ppermute | solution.py:16
  47.9 6.7 %collective-permute-start.1 = (bf16[8,16,128]{2,1,0:T(8,128)(2,1)S(1)}, bf16[8,16,128]{2,1,0:T(8,128)(2,1)S(1)}, u32[]{:S(2)}, u32[]{:S(2)}) collective-permute-start(bf16[8,16,128]{2,1,0:T(8,128)(2,1)S(1)} %fusion.57), channel_id=1, source_target_pairs={{0,4},{4,8},{8,12},{12,16},{16,20},{20,24},{24,28},{1,5},{5,9},{9,... | collective-permute-start | bytes 98312 | tf_op jit(solution)/shard_map/while/body/eval_jaxpr/ppermute | solution.py:16
  56.5 16.1 %collective-permute-start.2 = (bf16[8,128]{1,0:T(8,128)(2,1)S(1)}, bf16[8,128]{1,0:T(8,128)(2,1)S(1)}, u32[]{:S(2)}, u32[]{:S(2)}) collective-permute-start(bf16[8,128]{1,0:T(8,128)(2,1)S(1)} %fusion.58), channel_id=1, source_target_pairs={{0,4},{4,8},{8,12},{12,16},{16,20},{20,24},{24,28},{1,5},{5,9},{9,... | collective-permute-start | bytes 6152 | tf_op jit(solution)/shard_map/while/body/eval_jaxpr/ppermute | solution.py:16
  60.8 12.3 %collective-permute-start = (bf16[8,256,128]{2,1,0:T(8,128)(2,1)}, bf16[8,256,128]{2,1,0:T(8,128)(2,1)}, u32[]{:S(2)}, u32[]{:S(2)}) collective-permute-start(bf16[8,256,128]{2,1,0:T(8,128)(2,1)} %fusion.56), channel_id=1, source_target_pairs={{0,4},{4,8},{8,12},{12,16},{16,20},{20,24},{24,28},{1,5},{5,9},{9,... | collective-permute-start | bytes 1572872 | tf_op jit(solution)/shard_map/while/body/eval_jaxpr/ppermute | solution.py:16
  65.8 7.3 %collective-permute-start.3 = (bf16[8,256]{1,0:T(8,128)(2,1)S(1)}, bf16[8,256]{1,0:T(8,128)(2,1)S(1)}, u32[]{:S(2)}, u32[]{:S(2)}) collective-permute-start(bf16[8,256]{1,0:T(8,128)(2,1)S(1)} %fusion.59), channel_id=1, source_target_pairs={{0,4},{4,8},{8,12},{12,16},{16,20},{20,24},{24,28},{1,5},{5,9},{9,... | collective-permute-start | bytes 12296 | tf_op jit(solution)/shard_map/while/body/eval_jaxpr/ppermute | solution.py:16
  75.0 14.9 %collective-permute-start.2 = (bf16[8,128]{1,0:T(8,128)(2,1)S(1)}, bf16[8,128]{1,0:T(8,128)(2,1)S(1)}, u32[]{:S(2)}, u32[]{:S(2)}) collective-permute-start(bf16[8,128]{1,0:T(8,128)(2,1)S(1)} %fusion.58), channel_id=1, source_target_pairs={{0,4},{4,8},{8,12},{12,16},{16,20},{20,24},{24,28},{1,5},{5,9},{9,... | collective-permute-start | bytes 6152 | tf_op jit(solution)/shard_map/while/body/eval_jaxpr/ppermute | solution.py:16
  78.1 12.3 %collective-permute-start = (bf16[8,256,128]{2,1,0:T(8,128)(2,1)}, bf16[8,256,128]{2,1,0:T(8,128)(2,1)}, u32[]{:S(2)}, u32[]{:S(2)}) collective-permute-start(bf16[8,256,128]{2,1,0:T(8,128)(2,1)} %fusion.56), channel_id=1, source_target_pairs={{0,4},{4,8},{8,12},{12,16},{16,20},{20,24},{24,28},{1,5},{5,9},{9,... | collective-permute-start | bytes 1572872 | tf_op jit(solution)/shard_map/while/body/eval_jaxpr/ppermute | solution.py:16
  82.7 7.7 %collective-permute-start.3 = (bf16[8,256]{1,0:T(8,128)(2,1)S(1)}, bf16[8,256]{1,0:T(8,128)(2,1)S(1)}, u32[]{:S(2)}, u32[]{:S(2)}) collective-permute-start(bf16[8,256]{1,0:T(8,128)(2,1)S(1)} %fusion.59), channel_id=1, source_target_pairs={{0,4},{4,8},{8,12},{12,16},{16,20},{20,24},{24,28},{1,5},{5,9},{9,... | collective-permute-start | bytes 12296 | tf_op jit(solution)/shard_map/while/body/eval_jaxpr/ppermute | solution.py:16
  92.3 14.9 %collective-permute-start.2 = (bf16[8,128]{1,0:T(8,128)(2,1)S(1)}, bf16[8,128]{1,0:T(8,128)(2,1)S(1)}, u32[]{:S(2)}, u32[]{:S(2)}) collective-permute-start(bf16[8,128]{1,0:T(8,128)(2,1)S(1)} %fusion.58), channel_id=1, source_target_pairs={{0,4},{4,8},{8,12},{12,16},{16,20},{20,24},{24,28},{1,5},{5,9},{9,... | collective-permute-start | bytes 6152 | tf_op jit(solution)/shard_map/while/body/eval_jaxpr/ppermute | solution.py:16
  95.5 12.3 %collective-permute-start = (bf16[8,256,128]{2,1,0:T(8,128)(2,1)}, bf16[8,256,128]{2,1,0:T(8,128)(2,1)}, u32[]{:S(2)}, u32[]{:S(2)}) collective-permute-start(bf16[8,256,128]{2,1,0:T(8,128)(2,1)} %fusion.56), channel_id=1, source_target_pairs={{0,4},{4,8},{8,12},{12,16},{16,20},{20,24},{24,28},{1,5},{5,9},{9,... | collective-permute-start | bytes 1572872 | tf_op jit(solution)/shard_map/while/body/eval_jaxpr/ppermute | solution.py:16
  100.1 7.7 %collective-permute-start.3 = (bf16[8,256]{1,0:T(8,128)(2,1)S(1)}, bf16[8,256]{1,0:T(8,128)(2,1)S(1)}, u32[]{:S(2)}, u32[]{:S(2)}) collective-permute-start(bf16[8,256]{1,0:T(8,128)(2,1)S(1)} %fusion.59), channel_id=1, source_target_pairs={{0,4},{4,8},{8,12},{12,16},{16,20},{20,24},{24,28},{1,5},{5,9},{9,... | collective-permute-start | bytes 12296 | tf_op jit(solution)/shard_map/while/body/eval_jaxpr/ppermute | solution.py:16
  109.7 14.9 %collective-permute-start.2 = (bf16[8,128]{1,0:T(8,128)(2,1)S(1)}, bf16[8,128]{1,0:T(8,128)(2,1)S(1)}, u32[]{:S(2)}, u32[]{:S(2)}) collective-permute-start(bf16[8,128]{1,0:T(8,128)(2,1)S(1)} %fusion.58), channel_id=1, source_target_pairs={{0,4},{4,8},{8,12},{12,16},{16,20},{20,24},{24,28},{1,5},{5,9},{9,... | collective-permute-start | bytes 6152 | tf_op jit(solution)/shard_map/while/body/eval_jaxpr/ppermute | solution.py:16
  112.8 12.3 %collective-permute-start = (bf16[8,256,128]{2,1,0:T(8,128)(2,1)}, bf16[8,256,128]{2,1,0:T(8,128)(2,1)}, u32[]{:S(2)}, u32[]{:S(2)}) collective-permute-start(bf16[8,256,128]{2,1,0:T(8,128)(2,1)} %fusion.56), channel_id=1, source_target_pairs={{0,4},{4,8},{8,12},{12,16},{16,20},{20,24},{24,28},{1,5},{5,9},{9,... | collective-permute-start | bytes 1572872 | tf_op jit(solution)/shard_map/while/body/eval_jaxpr/ppermute | solution.py:16
  117.4 7.7 %collective-permute-start.3 = (bf16[8,256]{1,0:T(8,128)(2,1)S(1)}, bf16[8,256]{1,0:T(8,128)(2,1)S(1)}, u32[]{:S(2)}, u32[]{:S(2)}) collective-permute-start(bf16[8,256]{1,0:T(8,128)(2,1)S(1)} %fusion.59), channel_id=1, source_target_pairs={{0,4},{4,8},{8,12},{12,16},{16,20},{20,24},{24,28},{1,5},{5,9},{9,... | collective-permute-start | bytes 12296 | tf_op jit(solution)/shard_map/while/body/eval_jaxpr/ppermute | solution.py:16
  118.7 6.4 %collective-permute-start.1 = (bf16[8,16,128]{2,1,0:T(8,128)(2,1)S(1)}, bf16[8,16,128]{2,1,0:T(8,128)(2,1)S(1)}, u32[]{:S(2)}, u32[]{:S(2)}) collective-permute-start(bf16[8,16,128]{2,1,0:T(8,128)(2,1)S(1)} %fusion.57), channel_id=1, source_target_pairs={{0,4},{4,8},{8,12},{12,16},{16,20},{20,24},{24,28},{1,5},{5,9},{9,... | collective-permute-start | bytes 98312 | tf_op jit(solution)/shard_map/while/body/eval_jaxpr/ppermute | solution.py:16
  127.0 14.9 %collective-permute-start.2 = (bf16[8,128]{1,0:T(8,128)(2,1)S(1)}, bf16[8,128]{1,0:T(8,128)(2,1)S(1)}, u32[]{:S(2)}, u32[]{:S(2)}) collective-permute-start(bf16[8,128]{1,0:T(8,128)(2,1)S(1)} %fusion.58), channel_id=1, source_target_pairs={{0,4},{4,8},{8,12},{12,16},{16,20},{20,24},{24,28},{1,5},{5,9},{9,... | collective-permute-start | bytes 6152 | tf_op jit(solution)/shard_map/while/body/eval_jaxpr/ppermute | solution.py:16
  130.2 12.3 %collective-permute-start = (bf16[8,256,128]{2,1,0:T(8,128)(2,1)}, bf16[8,256,128]{2,1,0:T(8,128)(2,1)}, u32[]{:S(2)}, u32[]{:S(2)}) collective-permute-start(bf16[8,256,128]{2,1,0:T(8,128)(2,1)} %fusion.56), channel_id=1, source_target_pairs={{0,4},{4,8},{8,12},{12,16},{16,20},{20,24},{24,28},{1,5},{5,9},{9,... | collective-permute-start | bytes 1572872 | tf_op jit(solution)/shard_map/while/body/eval_jaxpr/ppermute | solution.py:16
  134.7 7.7 %collective-permute-start.3 = (bf16[8,256]{1,0:T(8,128)(2,1)S(1)}, bf16[8,256]{1,0:T(8,128)(2,1)S(1)}, u32[]{:S(2)}, u32[]{:S(2)}) collective-permute-start(bf16[8,256]{1,0:T(8,128)(2,1)S(1)} %fusion.59), channel_id=1, source_target_pairs={{0,4},{4,8},{8,12},{12,16},{16,20},{20,24},{24,28},{1,5},{5,9},{9,... | collective-permute-start | bytes 12296 | tf_op jit(solution)/shard_map/while/body/eval_jaxpr/ppermute | solution.py:16
  144.3 14.9 %collective-permute-start.2 = (bf16[8,128]{1,0:T(8,128)(2,1)S(1)}, bf16[8,128]{1,0:T(8,128)(2,1)S(1)}, u32[]{:S(2)}, u32[]{:S(2)}) collective-permute-start(bf16[8,128]{1,0:T(8,128)(2,1)S(1)} %fusion.58), channel_id=1, source_target_pairs={{0,4},{4,8},{8,12},{12,16},{16,20},{20,24},{24,28},{1,5},{5,9},{9,... | collective-permute-start | bytes 6152 | tf_op jit(solution)/shard_map/while/body/eval_jaxpr/ppermute | solution.py:16
  147.5 12.3 %collective-permute-start = (bf16[8,256,128]{2,1,0:T(8,128)(2,1)}, bf16[8,256,128]{2,1,0:T(8,128)(2,1)}, u32[]{:S(2)}, u32[]{:S(2)}) collective-permute-start(bf16[8,256,128]{2,1,0:T(8,128)(2,1)} %fusion.56), channel_id=1, source_target_pairs={{0,4},{4,8},{8,12},{12,16},{16,20},{20,24},{24,28},{1,5},{5,9},{9,... | collective-permute-start | bytes 1572872 | tf_op jit(solution)/shard_map/while/body/eval_jaxpr/ppermute | solution.py:16
  152.1 7.7 %collective-permute-start.3 = (bf16[8,256]{1,0:T(8,128)(2,1)S(1)}, bf16[8,256]{1,0:T(8,128)(2,1)S(1)}, u32[]{:S(2)}, u32[]{:S(2)}) collective-permute-start(bf16[8,256]{1,0:T(8,128)(2,1)S(1)} %fusion.59), channel_id=1, source_target_pairs={{0,4},{4,8},{8,12},{12,16},{16,20},{20,24},{24,28},{1,5},{5,9},{9,... | collective-permute-start | bytes 12296 | tf_op jit(solution)/shard_map/while/body/eval_jaxpr/ppermute | solution.py:16
  (23 other events, 103.3 us)
Sparse Core Ops, SparseCore 0:
  187.1 77.6 reduce-scatter.1
where the time goes:
time: 273 us; the launch traced here: 272 us
  starting transfers between devices  93.7 us (34%)
  waiting for transfers between devices  83.5 us (31%)
  matrix products  45.7 us (17%)
  other arithmetic  32.2 us (12%)
  between operations  13.6 us (5%)
    ppermute x35, starting transfers between devices, passed_along(): return lax.ppermute(block, axis, route)  93.7 us
    reduce_scatter x1, waiting for transfers between devices, per_device(): lax.psum_scatter(partial_value.astype(jnp.bfloat16), 'tp', scatter_dimens...  77.8 us
    dot_general x3, matrix products, project(): jnp.dot(inputs, weight, preferred_element_type=jnp.float32) * factor  16.2 us
    dot_general x1, matrix products, per_device(): jnp.dot(normalized, out_weight, preferred_element_type=jnp.float32)  9.5 us
    convert_element_type x7, other arithmetic, relay(): passed_along(summed[0].astype(jnp.bfloat16), 'ctx', 1).astype(jnp.float32)  7.78 us
    convert_element_type x7, other arithmetic, relay(): summed[0].astype(jnp.bfloat16)  6.45 us
    ppermute x35, waiting for transfers between devices, passed_along(): return lax.ppermute(block, axis, route)  5.69 us
  transfers between devices with their start and end apart: 36, of which 8 were waited for; matrix products, arithmetic and copies ran while one was open for 4% of the time, Pallas kernels for 0%

commit v1 on v0

v1 whole, which is shorter than its diff:
```python
import functools

import jax
import jax.numpy as jnp
from jax import lax
from jax.experimental import pallas as pl
from jax.experimental.pallas import tpu as pltpu
from jax.sharding import PartitionSpec as P

F = 16
DV = 128
ROLLS = F // 2
FEATURES = 2 * F + (ROLLS - 1) * F + F
HALF_ROOT = 0.7071067811865476
DEPTH_TILE = 1024
AHEAD = 2
PIECES = 1
VMEM_LIMIT = 24 * 1024 * 1024
NT = (((1,), (1,)), ((), ()))
f32 = jnp.float32
bf16 = jnp.bfloat16


def feature_blocks(x, double):
    tokens = x.shape[1]
    blocks = [x, x * x * HALF_ROOT]
    for d in range(1, ROLLS + 1):
        rolled = jnp.concatenate([x[d:], x[:d]], axis=0)
        block = x * rolled * HALF_ROOT
        if double:
            block = block * 2.0
        blocks.append(block)
    row = lax.broadcasted_iota(jnp.int32, (F // 2, tokens), 0)
    tail = jnp.where(row == 0, 1.0, 0.0).astype(f32)
    blocks[-1] = jnp.concatenate([blocks[-1][: F // 2], tail], axis=0)
    return blocks


def in_hbm(x):
    return pltpu.with_memory_space_constraint(x, pltpu.HBM)


def in_vmem(x):
    return pltpu.with_memory_space_constraint(x, pltpu.VMEM)


def call(kernel, outputs, flops, *, smem=(), vmem=(), free=(), hbm=(), loose=(), **options):
    block = pl.BlockSpec(memory_space=pltpu.VMEM)
    raw = pl.BlockSpec(memory_space=pl.ANY)
    spaces = {"vmem": pltpu.VMEM, "hbm": pltpu.HBM, "free": jax.ShapeDtypeStruct, "raw": pltpu.HBM}
    return pl.pallas_call(
        kernel,
        in_specs=[pl.BlockSpec(memory_space=pltpu.SMEM)] * len(smem)
        + [block] * (len(vmem) + len(free))
        + [raw] * (len(hbm) + len(loose)),
        out_specs=[raw if place == "raw" else block for _, _, place in outputs],
        out_shape=[spaces[place](shape, kind) for shape, kind, place in outputs],
        compiler_params=pltpu.CompilerParams(vmem_limit_bytes=VMEM_LIMIT),
        cost_estimate=pl.CostEstimate(flops=flops, bytes_accessed=flops // 256, transcendentals=0),
        **options,
    )(*[x.reshape(1) for x in smem], *[in_vmem(x) for x in vmem], *free, *[in_hbm(x) for x in hbm], *loose)


def depth_chunks(depth):
    size = min(DEPTH_TILE, depth)
    edges = [0, size // 2] + list(range(size, depth + 1, size))
    return [(start, stop - start) for start, stop in zip(edges, edges[1:])]


def project_kernel(tokens, wq, wk, wv, q_out, k_out, v_out, state, x, w_q, w_k, w_v, acc_qk, acc_v, key_features, sems):
    rows, depth = tokens.shape
    width = wq.shape[1]
    heads = width // F
    chunks = depth_chunks(depth)
    halves = (slice(0, rows // 2), slice(rows // 2, rows))

    def copies(c):
        if c >= len(chunks):
            return ()
        begin, size = chunks[c]
        part = pl.ds(begin, size)
        pairs = [(wk.at[part, :], w_k.at[part, :]), (wq.at[part, :], w_q.at[part, :])]
        for i in range(PIECES):
            some = pl.ds(i * rows // PIECES, rows // PIECES)
            pairs.append((tokens.at[some, part], x.at[some, part]))
            some = pl.ds(begin + i * size // PIECES, size // PIECES)
            pairs.append((wv.at[some, :], w_v.at[some, :]))
        return [pltpu.make_async_copy(*pair, sems.at[c, i]) for i, pair in enumerate(pairs)]

    def start(c):
        for copy in copies(c):
            copy.start()

    for c in range(AHEAD):
        start(c)
    for c, (begin, size) in enumerate(chunks):
        for copy in copies(c):
            copy.wait()
        start(c + AHEAD)
        part = slice(begin, begin + size)
        w = jnp.concatenate([w_k[part, :], w_q[part, :]], axis=1)
        for some in halves:
            qk = jnp.dot(x[some, part], w, preferred_element_type=f32)
            values = jnp.dot(x[some, part], w_v[part, :], preferred_element_type=f32)
            if c == 0:
                acc_qk[some, :] = qk
                acc_v[some, :] = values
            elif c < len(chunks) - 1:
                acc_qk[some, :] += qk
                acc_v[some, :] += values
            else:
                acc_qk[some, :] += qk
                v_out[some, :] = (acc_v[some, :] + values).astype(bf16)
    both = (acc_qk[...] * F ** (-0.25)).astype(bf16)
    keys = both[:, :width]
    k_out[...] = keys
    q_out[...] = both[:, width:]
    turned = keys.astype(f32).T
    for h in range(heads):
        for b, block in enumerate(feature_blocks(turned[h * F : (h + 1) * F], False)):
            key_features[h, b * F : (b + 1) * F, :] = block.astype(bf16)
    ones = jnp.ones((rows, DV), bf16)
    lane = lax.broadcasted_iota(jnp.int32, (FEATURES, DV), 1)
    sums = jnp.zeros((FEATURES, DV), f32)
    for h in range(heads):
        wide = jnp.concatenate([v_out[:, h * DV : (h + 1) * DV], ones], axis=1)
        total = jnp.dot(key_features[h], wide, preferred_element_type=f32)
        state[h * FEATURES : (h + 1) * FEATURES, :] = total[:, :DV].astype(bf16)
        sums = jnp.where(lane == h, total[:, DV:], sums)
    turned_sums = sums.T
    low = turned_sums[:8, :128]
    high = jnp.concatenate([turned_sums[:8, 128:], jnp.zeros((8, 256 - FEATURES), f32)], axis=1)
    state[heads * FEATURES :, :] = jnp.concatenate([low, high], axis=0).astype(bf16)


def project(tokens, wq, wk, wv):
    rows, depth = tokens.shape
    heads = wv.shape[1] // DV
    width = heads * F
    shapes = [(rows, width), (rows, width), (rows, heads * DV), (heads * FEATURES + 16, DV)]
    return call(
        project_kernel,
        [(shape, bf16, "vmem") for shape in shapes],
        2 * rows * depth * heads * (DV + 2 * F),
        hbm=[tokens, wq, wk, wv],
        scratch_shapes=[
            pltpu.VMEM((rows, depth), bf16),
            pltpu.VMEM((depth, width), bf16),
            pltpu.VMEM((depth, width), bf16),
            pltpu.VMEM((depth, heads * DV), bf16),
            pltpu.VMEM((rows, 2 * width), f32),
            pltpu.VMEM((rows, heads * DV), f32),
            pltpu.VMEM((heads, FEATURES, rows), bf16),
            pltpu.SemaphoreType.DMA((len(depth_chunks(depth)), 2 + 2 * PIECES)),
        ],
    )


def local_kernel(start, q, k, v, numerators, denominators, features):
    rows = q.shape[0]
    turned = q[...].astype(f32).T
    for i in range(features.shape[0]):
        blocks = feature_blocks(turned[(start + i) * F : (start + i + 1) * F], True)
        features[i] = jnp.concatenate(blocks, axis=0).T.astype(bf16)
    half = rows // 2
    lane = lax.broadcasted_iota(jnp.int32, q.shape, 1)
    row = lax.broadcasted_iota(jnp.int32, (half, half), 0)
    column = lax.broadcasted_iota(jnp.int32, (half, half), 1)
    queries = q[...]
    keys = k[...]
    ones = jnp.ones((rows, DV), bf16)
    wide_lane = lax.broadcasted_iota(jnp.int32, (half, DV), 1)
    sums = [jnp.zeros((half, DV), f32)] * 2
    for i in range(numerators.shape[1] // DV):
        h = start + i
        mine = jnp.where(lane // F == h, queries, jnp.zeros_like(queries))
        values = jnp.concatenate([v[:, h * DV : (h + 1) * DV], ones], axis=1)

        def weights(top, left):
            r = lax.dot_general(
                mine[top * half : (top + 1) * half],
                keys[left * half : (left + 1) * half],
                NT,
                preferred_element_type=f32,
            )
            w = 1.0 + r + r * r * 0.5
            if top == left:
                w = jnp.where(column <= row, w, 0.0)
            return w.astype(bf16)

        upper = jnp.dot(weights(0, 0), values[:half], preferred_element_type=f32)
        lower = jnp.concatenate([weights(1, 0), weights(1, 1)], axis=1)
        lower = jnp.dot(lower, values, preferred_element_type=f32)
        for j, both in enumerate((upper, lower)):
            numerators[j * half : (j + 1) * half, i * DV : (i + 1) * DV] = both[:, :DV].astype(bf16)
            sums[j] = jnp.where(wide_lane == i, both[:, DV:], sums[j])
    for j in range(2):
        denominators[j * half : (j + 1) * half] = sums[j]


def local_attention(q, k, v, start, count):
    rows = q.shape[0]
    return call(
        functools.partial(local_kernel, start),
        [
            ((rows, count * DV), bf16, "hbm"),
            ((rows, DV), f32, "hbm"),
            ((count, rows, FEATURES), bf16, "hbm"),
        ],
        count * 4 * rows * rows * 2 * DV,
        vmem=[q, k, v],
    )


def finish_kernel(begin, shards, rounds, parts, *refs):
    me, chunk, gain, *refs = refs
    received, (w, *refs) = refs[:rounds], refs[rounds:]
    sources, (normalized, out) = refs[: 3 * parts], refs[-9:-7]
    held_features, held_numerators, held_denominators, held_w, wide, products, sems = refs[-7:]
    heads, rows, _ = held_features.shape
    split = heads // parts
    width = out.shape[1]
    part = pl.ds(begin, rows)
    columns = pl.ds(pl.multiple_of(chunk[0] * width, 128), width)
    early = []

    def fetch(source, target):
        early.append(pltpu.make_async_copy(source, target, sems.at[len(early)]))

    for i in range(parts):
        numerators, denominators, features = sources[3 * i : 3 * i + 3]
        fetch(features.at[:, part, :], held_features.at[pl.ds(i * split, split)])
        fetch(numerators.at[part, :], held_numerators.at[i])
        fetch(denominators.at[part, :], held_denominators.at[i])
    late = []
    for i in range(PIECES):
        some = pl.ds(i * (w.shape[0] // PIECES), w.shape[0] // PIECES)
        late.append(pltpu.make_async_copy(w.at[some, columns], held_w.at[some, :], sems.at[3 * parts + i]))
    for copy in early + late:
        copy.start()

    sums, states = prefix_states(shards, me[0], heads, received)
    sums = jnp.concatenate([sums[:8], sums[8:, : FEATURES - 128]], axis=1)
    sums = jnp.concatenate([sums, jnp.zeros((DV - 8, FEATURES), f32)], axis=0).T
    prefixes = []
    for h in range(heads):
        wide_sums = jnp.broadcast_to(sums[:, h : h + 1], (FEATURES, DV))
        prefixes.append(jnp.concatenate([states(h), wide_sums], axis=1).astype(bf16))
    for copy in early:
        copy.wait()
    for h in range(heads):
        products[h] = jnp.dot(held_features[h], prefixes[h], preferred_element_type=f32)
    spreads = []
    for h in range(heads):
        p, i = h // split, h % split
        numerator = products[h, :, :DV] + held_numerators[p, :, i * DV : (i + 1) * DV].astype(f32)
        denominator = products[h, :, DV:] + held_denominators[p, :, i : i + 1]
        products[h, :, :DV] = numerator / denominator
    for h in range(heads):
        ratio = products[h, :, :DV]
        spreads.append(jnp.mean(ratio * ratio, axis=1, keepdims=True))
    for h in range(heads):
        columns = slice(h * DV, (h + 1) * DV)
        scaled = products[h, :, :DV] * lax.rsqrt(spreads[h] + 1e-06) * gain[columns].astype(f32).reshape(1, DV)
        wide[:, columns] = scaled.astype(bf16)
    normalized[...] = wide[...]
    for copy in late:
        copy.wait()
    out[...] = jnp.dot(wide[...], held_w[...], preferred_element_type=f32).astype(bf16)


def finish(shards, me, chunk, gain, w, local, received, begin, rows, width, after):
    heads = sum(features.shape[0] for _, _, features in local)
    parts = len(local)
    return call(
        functools.partial(finish_kernel, begin, shards, len(received), parts),
        [((rows, heads * DV), bf16, "hbm"), ((rows, width), bf16, "free")],
        2 * heads * rows * (256 * 256 + DV * width),
        smem=[me, chunk],
        free=[gain, *received],
        hbm=[w, *[array for arrays in local for array in arrays]],
        loose=after,
        scratch_shapes=[
            pltpu.VMEM((heads, rows, FEATURES), bf16),
            pltpu.VMEM((parts, rows, heads // parts * DV), bf16),
            pltpu.VMEM((parts, rows, DV), f32),
            pltpu.VMEM((w.shape[0], width), bf16),
            pltpu.VMEM((rows, heads * DV), bf16),
            pltpu.VMEM((heads, rows, 2 * DV), f32),
            pltpu.SemaphoreType.DMA((3 * parts + PIECES,)),
        ],
    )


def partials_kernel(*refs):
    w, normalized, out = refs[:PIECES], refs[PIECES:-1], refs[-1]
    begin = 0
    w = jnp.concatenate([piece[...] for piece in w], axis=0)
    for block in normalized:
        rows = block.shape[0]
        out[0, begin : begin + rows] = jnp.dot(block[...], w, preferred_element_type=f32).astype(bf16)
        begin += rows


def partials(normalized, w, count):
    depth, columns = w.shape
    tile = columns // count
    rows = sum(block.shape[0] for block in normalized)
    whole = lambda a: pl.BlockSpec(a.shape, lambda i: (0,) * a.ndim)
    piece = lambda p: pl.BlockSpec((depth // PIECES, tile), lambda i: (p, i))
    return pl.pallas_call(
        partials_kernel,
        grid=(count,),
        in_specs=[piece(p) for p in range(PIECES)] + [whole(block) for block in normalized],
        out_specs=pl.BlockSpec((1, rows, tile), lambda i: (i, 0, 0)),
        out_shape=pltpu.HBM((count, rows, tile), bf16),
        compiler_params=pltpu.CompilerParams(vmem_limit_bytes=VMEM_LIMIT),
        cost_estimate=pl.CostEstimate(
            flops=2 * rows * depth * columns, bytes_accessed=2 * depth * columns, transcendentals=0
        ),
    )(*[in_hbm(w)] * PIECES, *[in_hbm(block) for block in normalized])


def messages_kernel(begin, count, *refs):
    chunks, refs = refs[:count], refs[count:]
    up, down, sums, *refs = refs
    *outs, held, sems = refs[-count - 2 :]
    rows = up.shape[0]
    copies = []
    for i, chunk in enumerate(chunks):
        copies.append(pltpu.make_async_copy(sums.at[chunk[0], pl.ds(begin, rows), :], held.at[i], sems.at[i]))
        copies[i].start()
    for i, (received, out) in enumerate(zip((up, down, None), outs)):
        copies[i].wait()
        out[...] = held[i] if received is None else (held[i].astype(f32) + received[...].astype(f32)).astype(bf16)


def messages(sums, chunks, up, down, begin, after):
    count = len(chunks)
    return call(
        functools.partial(messages_kernel, begin, count),
        [(up.shape, bf16, "free")] * count,
        up.size * 256,
        smem=chunks,
        free=[up, down],
        hbm=[sums],
        loose=after,
        scratch_shapes=[pltpu.VMEM((count, *up.shape), bf16), pltpu.SemaphoreType.DMA((count,))],
    )


def final_kernel(begin, own, up, down, *rest):
    out, held, sems = rest[-3:]
    rows = up.shape[0]
    middle = rows // 32 * 16
    copies = []
    for i, (start, size) in enumerate(((0, middle), (middle, rows - middle))):
        part = slice(start, start + size)
        total = own[part].astype(f32) + up[part].astype(f32) + down[part].astype(f32)
        held[part] = total.astype(bf16)
        target = out.at[pl.ds(begin + start, size), :]
        copies.append(pltpu.make_async_copy(held.at[pl.ds(start, size), :], target, sems.at[i]))
        copies[-1].start()
    for copy in copies:
        copy.wait()


def final(own, up, down, begin, rows, output):
    width = up.shape[1]
    earlier = [] if output is None else [output]
    return call(
        functools.partial(final_kernel, begin),
        [((rows, width), bf16, "raw")],
        rows * width * 64,
        free=[own, up, down],
        hbm=earlier,
        input_output_aliases={3: 0} if earlier else {},
        scratch_shapes=[pltpu.VMEM(up.shape, bf16), pltpu.SemaphoreType.DMA((2,))],
    )[0]


def reduced(first, w, rows, edges):
    line = lax.axis_size("tp")
    place = lax.axis_index("tp")
    top = line - 1

    def chunk(index):
        return jnp.clip(index, 0, top).astype(jnp.int32)

    def send(block, pairs):
        return lax.ppermute(block, "tp", pairs)

    ups = [[(z, z + 1) for z in range(step + 1)] for step in range(top)]
    downs = [[(top - z, top - z - 1) for z in range(step + 1)] for step in range(top)]
    blocks = list(zip(edges, edges[1:]))
    normalized, own, up, down = [[None] * len(blocks) for _ in range(4)]
    after = []
    for b, (begin, stop) in enumerate(blocks):
        normalized[b], sums = first(begin, stop - begin, chunk(jnp.where(place < line // 2, top, 0)), after)
        up[b] = down[b] = send(sums, ups[0] + downs[0])
        after = [sums]
    sums = partials(normalized, w, line)
    after = []
    for step in range(1, top):
        chunks = [chunk(top - step + place), chunk(place - top + step)] + ([chunk(place)] if step == top - 1 else [])
        for b, (begin, _) in enumerate(blocks):
            after = messages(sums, chunks, up[b], down[b], begin, after[:2])
            up[b], down[b] = send(after[0], ups[step]), send(after[1], downs[step])
            own[b] = after[-1]
    output = None
    for b, (begin, _) in enumerate(blocks):
        output = final(own[b], up[b], down[b], begin, rows, output)
    return output


def bit_of(me, bit):
    return ((me >> bit) & 1).astype(f32)


def join_kernel(me, mine, other, out):
    size = out.shape[0] - 16

    def read(start, count):
        part = slice(start, start + count)
        return mine[part].astype(f32) + other[part].astype(f32)

    out[:size] = jnp.where((me[0] & 1) == 1, read(size, size), read(0, size)).astype(bf16)
    out[size:] = read(2 * size, 16).astype(bf16)


def cross_kernel(high_bit, me, mine, other, out):
    odd, low, high = bit_of(me[0], 0), bit_of(me[0], high_bit - 1), bit_of(me[0], high_bit)
    own = mine[...].astype(f32) * ((1.0 - odd) + odd * (1.0 - low))
    out[...] = (own + other[...].astype(f32) * ((1.0 - odd) + odd * high)).astype(bf16)


def add_kernel(me, mine, other, out):
    out[...] = (mine[...].astype(f32) + other[...].astype(f32)).astype(bf16)


def earlier_kernel(bits, me, *refs):
    *received, out = refs
    total = jnp.zeros(out.shape, f32)
    for piece, coefficient in zip(received, half_coefficients(me[0], bits)):
        total = total + piece[...].astype(f32) * coefficient
    out[...] = total.astype(bf16)


def half_coefficients(me, bits):
    if bits < 3:
        return [bit_of(me, bit) for bit in range(1, bits)]
    odd, low, high = bit_of(me, 0), bit_of(me, bits - 2), bit_of(me, bits - 1)
    return [bit_of(me, bit) for bit in range(1, bits - 2)] + [
        (1.0 - odd) * low + odd * high,
        (1.0 - odd) * high + odd * jnp.maximum(low, high),
    ]


def prefix_states(shards, me, heads, received):
    first, mine, others = received
    size = heads // 2 * FEATURES
    odd = (me & 1) == 1
    coefficient = bit_of(me, 0)
    sums = first[2 * size : 2 * size + 16].astype(f32) * coefficient + mine[size:].astype(f32)

    def states(h):
        part = slice(h * FEATURES, (h + 1) * FEATURES)
        at = slice(h * FEATURES % size, h * FEATURES % size + FEATURES)
        low, high = mine[at].astype(f32), others[at].astype(f32)
        passed = jnp.where(odd, high, low) if h < heads // 2 else jnp.where(odd, low, high)
        return first[part].astype(f32) * coefficient + passed

    return sums, states


def exchange_rounds(shards):
    bits = shards.bit_length() - 1
    if bits < 3:
        return [[bit] * shards for bit in range(1, bits)]
    rounds = [[bit] * shards for bit in range(1, bits - 2)]
    rounds.append([bits - 1 if i & 1 else bits - 2 for i in range(shards)])
    rounds.append([bits - 2 if i & 1 else bits - 1 for i in range(shards)])
    return rounds


def per_device(tokens, query_weight, key_weight, value_weight, norm_gain, out_weight):
    rows = tokens.shape[0]
    heads = norm_gain.shape[0] // DV
    shards, line = lax.axis_size("ctx"), lax.axis_size("tp")
    me = lax.axis_index("ctx")
    bits = shards.bit_length() - 1
    plan = exchange_rounds(shards)
    q, k, v, states = project(tokens, query_weight, key_weight, value_weight)

    def swap(block, across):
        return lax.ppermute(block, "ctx", [(i, i ^ (1 << across[i])) for i in range(shards)])

    def small(kernel, operands, shape):
        return call(kernel, [(shape, bf16, "vmem")], shape[0] * shape[1] * 64, smem=[me], vmem=operands)[0]

    half = heads // 2
    shape = (half * FEATURES + 16, DV)
    first = swap(states, [0] * shards)
    passed = small(join_kernel, [states, first], shape)
    local, halves = [], []
    for turn, across in enumerate(plan):
        other = swap(passed, across)
        if len(local) < 2:
            local.append(local_attention(q, k, v, len(local) * half, half))
        halves.append(other)
        if turn < len(plan) - 1:
            kernel = functools.partial(cross_kernel, bits - 1) if turn == bits - 3 else add_kernel
            passed = small(kernel, [passed, other], shape)
            q, k, v, passed, local = lax.optimization_barrier((q, k, v, passed, local))
    while len(local) < 2:
        local.append(local_attention(q, k, v, len(local) * half, half))
    halves, local = lax.optimization_barrier((halves, local))
    mine = small(functools.partial(earlier_kernel, bits), halves, shape)
    received = [first, mine, swap(mine, [0] * shards)]
    width = out_weight.shape[1] // line

    def begin_block(begin, size, chunk, after):
        return finish(shards, me, chunk, norm_gain, out_weight, local, received, begin, size, width, after)

    return reduced(begin_block, out_weight, rows, [0, rows // 2, rows])


def solution(mesh):
    in_specs = (P("ctx", None), P(None, "tp"), P(None, "tp"), P(None, "tp"), P("tp"), P("tp", None))
    out_specs = P("ctx", "tp")
    return jax.shard_map(
        per_device, mesh=mesh, in_specs=in_specs, out_specs=out_specs, check_vma=False
    )
```

time: 273 us -> 101 us (0.37)
  starting transfers between devices: 93.7 us -> 32.2 us
  waiting for transfers between devices: 83.5 us -> 28.7 us
  matrix products: 45.7 us -> 0 us
  Pallas kernels: 0 us -> 38.8 us
  other arithmetic: 32.2 us -> 0 us
  between operations: 13.6 us -> 0.36 us
    reduce_scatter x1 -> x0, waiting for transfers between devices: 77.8 us -> none  [per_device(): lax.psum_scatter(partial_value.astype(jnp.bfloat16), 'tp', scatter_dimens...]
    ppermute x35 -> x14, starting transfers between devices: 93.7 us -> 32.2 us  [the longest x10 26.5 us: send(): return lax.ppermute(block, 'tp', pairs)]
    dot_general x12 -> x0, matrix products: 45.7 us -> none  [the longest x3 16.2 us: project(): jnp.dot(inputs, weight, preferred_element_type=jnp.float32) * factor]
    pallas_call x0 -> x15, Pallas kernels: none -> 38.8 us  [the longest x14 30 us: call(): pl.pallas_call(kernel, in_specs=[pl.BlockSpec(memory_space=pltpu.SMEM)] *...]
    convert_element_type x73 -> x0, other arithmetic: 28.1 us -> none  [the longest x7 7.78 us: relay(): passed_along(summed[0].astype(jnp.bfloat16), 'ctx', 1).astype(jnp.float32)]
    ppermute x35 -> x14, waiting for transfers between devices: 5.69 us -> 28.7 us  [the longest x10 24.8 us: send(): return lax.ppermute(block, 'tp', pairs)]
  transfers between devices with their start and end apart: 36 -> 14, of which waited for: 8 -> 9; matrix products, arithmetic and copies ran while one was open for 4% -> 0% of each run, Pallas kernels for 0% -> 26%
where the time goes in v1:
time: 101 us; the launch traced here: 100 us
  Pallas kernels  38.8 us (38%)
  starting transfers between devices  32.2 us (32%)
  waiting for transfers between devices  28.7 us (28%)
    pallas_call x14, Pallas kernels, call(): pl.pallas_call(kernel, in_specs=[pl.BlockSpec(memory_space=pltpu.SMEM)] *...  30 us
    ppermute x10, starting transfers between devices, send(): return lax.ppermute(block, 'tp', pairs)  26.5 us
    ppermute x10, waiting for transfers between devices, send(): return lax.ppermute(block, 'tp', pairs)  24.8 us
    pallas_call x1, Pallas kernels, partials(): pl.pallas_call(partials_kernel, grid=(count,), in_specs=[piece(p) for p i...  8.76 us
    ppermute x4, starting transfers between devices, swap(): lax.ppermute(block, 'ctx', [(i, i ^ 1 << across[i]) for i in range(shards)])  5.63 us
    ppermute x4, waiting for transfers between devices, swap(): lax.ppermute(block, 'ctx', [(i, i ^ 1 << across[i]) for i in range(shards)])  3.92 us
  transfers between devices with their start and end apart: 14, of which 9 were waited for; matrix products, arithmetic and copies ran while one was open for 0% of the time, Pallas kernels for 26%

profile of v1, /device:TPU:0, one launch (start us, length us, event | category | flops | bytes accessed | tf_op | source)
XLA Modules:
  0.0 100.0 jit_solution(17149847500268670917)
XLA Ops:
  0.0 8.9 %shard_map.64 = (bf16[512,128]{1,0:T(8,128)(2,1)S(1)}, bf16[512,128]{1,0:T(8,128)(2,1)S(1)}, bf16[512,1024]{1,0:T(8,128)(2,1)S(1)}, bf16[1296,128]{1,0:T(8,128)(2,1)S(1)}) custom-call(bf16[512,4096]{1,0:T(8,128)(2,1)} %tokens.1, bf16[4096,128]{1,0:T(8,128)(2,1)} %wq.1, bf16[4096,128]{1,0:T(8,128)(2,1)} %wk.1, bf16[4096,1024]{1,0:T(8,128)(2,1)} %wv.1), custom_call_target="tpu_custom_call" | custom-call | flops 5368709120 | bytes 20971520 | tf_op jit(solution)/shard_map/pallas_call | solution.py:51
  10.7 2.9 %collective-permute-start.1 = (bf16[656,128]{1,0:T(8,128)(2,1)S(1)}, bf16[656,128]{1,0:T(8,128)(2,1)S(1)}, u32[]{:S(2)}, u32[]{:S(2)}) collective-permute-start(bf16[656,128]{1,0:T(8,128)(2,1)S(1)} %shard_map.65.mine), channel_id=1, source_target_pairs={{0,8},{4,20},{8,0},{12,28},{16,24},{20,4},{24,16},{28,12},{1,9},{5... | collective-permute-start | bytes 503816 | tf_op jit(solution)/shard_map/ppermute | solution.py:496
  13.7 2.7 %shard_map.67 = (bf16[512,512]{1,0:T(8,128)(2,1)}, f32[512,128]{1,0:T(8,128)}, bf16[4,512,160]{2,1,0:T(8,128)(2,1)}) custom-call(bf16[512,128]{1,0:T(8,128)(2,1)S(1)} %get-tuple-element.55.q, bf16[512,128]{1,0:T(8,128)(2,1)S(1)} %get-tuple-element.56.k, bf16[512,1024]{1,0:T(8,128)(2,1)S(1)} %get-tuple-element.57.v), custom_call_target="tpu_custom_call" | custom-call | flops 1073741824 | bytes 4194304 | tf_op jit(solution)/shard_map/pallas_call | solution.py:51
  17.1 2.1 %collective-permute-start.2 = (bf16[656,128]{1,0:T(8,128)(2,1)S(1)}, bf16[656,128]{1,0:T(8,128)(2,1)S(1)}, u32[]{:S(2)}, u32[]{:S(2)}) collective-permute-start(bf16[656,128]{1,0:T(8,128)(2,1)S(1)} %shard_map.66), channel_id=1, source_target_pairs={{0,16},{4,12},{8,24},{12,4},{16,0},{20,28},{24,8},{28,20},{1,17},{... | collective-permute-start | bytes 503816 | tf_op jit(solution)/shard_map/ppermute | solution.py:496
  19.2 2.7 %shard_map.68 = (bf16[512,512]{1,0:T(8,128)(2,1)}, f32[512,128]{1,0:T(8,128)}, bf16[4,512,160]{2,1,0:T(8,128)(2,1)}) custom-call(bf16[512,128]{1,0:T(8,128)(2,1)S(1)} %get-tuple-element.55.q, bf16[512,128]{1,0:T(8,128)(2,1)S(1)} %get-tuple-element.56.k, bf16[512,1024]{1,0:T(8,128)(2,1)S(1)} %get-tuple-element.57.v), custom_call_target="tpu_custom_call" | custom-call | flops 1073741824 | bytes 4194304 | tf_op jit(solution)/shard_map/pallas_call | solution.py:51
  22.7 1.4 %collective-permute-done.3.refs_5_ = bf16[656,128]{1,0:T(8,128)(2,1)S(1)} collective-permute-done((bf16[656,128]{1,0:T(8,128)(2,1)S(1)}, bf16[656,128]{1,0:T(8,128)(2,1)S(1)}, u32[]{:S(2)}, u32[]{:S(2)}) %collective-permute-start.3) | collective-permute-done | bytes 167968 | tf_op jit(solution)/shard_map/ppermute | solution.py:496
  24.1 3.2 %shard_map.70 = (bf16[256,1024]{1,0:T(8,128)(2,1)}, bf16[256,1024]{1,0:T(8,128)(2,1)S(1)}) custom-call(s32[1]{0:T(128)} %bitcast.5.me.refs_0_, s32[1]{0:T(128)} %bitcast.6.refs_1_, bf16[1024]{0:T(1024)(128)(2,1)S(1)} %copy-done, bf16[1296,128]{1,0:T(8,128)(2,1)S(1)} %collective-permute-done.other.refs_3_, bf16[656,128]{1,0:T(8,128)(2,1)S(1)} %shard_map.69.refs_4_, ...), custom_call_target="tpu_custom_call" | custom-call | flops 805306368 | bytes 3145728 | tf_op jit(solution)/shard_map/pallas_call | solution.py:51
  27.3 4.0 %collective-permute-start.5 = (bf16[256,1024]{1,0:T(8,128)(2,1)S(1)}, bf16[256,1024]{1,0:T(8,128)(2,1)S(1)}, u32[]{:S(2)}, u32[]{:S(2)}) collective-permute-start(bf16[256,1024]{1,0:T(8,128)(2,1)S(1)} %get-tuple-element.69.refs_13_), channel_id=1, source_target_pairs={{0,1},{3,2},{4,5},{7,6},{8,9},{11,10},{12,13},{15,14},{16,17},{19,... | collective-permute-start | bytes 1572872 | tf_op jit(solution)/shard_map/ppermute | solution.py:391
  31.3 3.2 %shard_map.71 = (bf16[256,1024]{1,0:T(8,128)(2,1)}, bf16[256,1024]{1,0:T(8,128)(2,1)S(1)}) custom-call(s32[1]{0:T(128)} %bitcast.5.me.refs_0_, s32[1]{0:T(128)} %bitcast.6.refs_1_, bf16[1024]{0:T(1024)(128)(2,1)S(1)} %copy-done, bf16[1296,128]{1,0:T(8,128)(2,1)S(1)} %collective-permute-done.other.refs_3_, bf16[656,128]{1,0:T(8,128)(2,1)S(1)} %shard_map.69.refs_4_, ...), custom_call_target="tpu_custom_call" | custom-call | flops 805306368 | bytes 3145728 | tf_op jit(solution)/shard_map/pallas_call | solution.py:51
  34.5 1.5 %collective-permute-start.4 = (bf16[256,1024]{1,0:T(8,128)(2,1)S(1)}, bf16[256,1024]{1,0:T(8,128)(2,1)S(1)}, u32[]{:S(2)}, u32[]{:S(2)}) collective-permute-start(bf16[256,1024]{1,0:T(8,128)(2,1)S(1)} %get-tuple-element.70), channel_id=1, source_target_pairs={{0,1},{3,2},{4,5},{7,6},{8,9},{11,10},{12,13},{15,14},{16,17},{19,... | collective-permute-start | bytes 1572872 | tf_op jit(solution)/shard_map/ppermute | solution.py:391
  36.1 8.8 %shard_map.72.refs_4_.refs_5_ = bf16[4,512,1024]{2,1,0:T(8,128)(2,1)} custom-call(bf16[1024,4096]{1,0:T(8,128)(2,1)} %refs_0_.1, bf16[256,1024]{1,0:T(8,128)(2,1)} %get-tuple-element.71.refs_1_, bf16[256,1024]{1,0:T(8,128)(2,1)} %get-tuple-element.72.refs_2_), custom_call_target="tpu_custom_call" | custom-call | flops 4294967296 | bytes 8388608 | tf_op jit(solution)/shard_map/pallas_call | solution.py:311
  44.8 2.0 %shard_map.73 = (bf16[256,1024]{1,0:T(8,128)(2,1)}, bf16[256,1024]{1,0:T(8,128)(2,1)S(1)}) custom-call(s32[1]{0:T(128)} %bitcast.3.refs_0_, s32[1]{0:T(128)} %bitcast.4.refs_1_, bf16[256,1024]{1,0:T(8,128)(2,1)S(1)} %collective-permute-done.5.refs_2_.refs_3_, bf16[256,1024]{1,0:T(8,128)(2,1)S(1)} %collective-permute-done.5.refs_2_.refs_3_, ...), custom_call_target="tpu_custom_call" | custom-call | flops 67108864 | bytes 262144 | tf_op jit(solution)/shard_map/pallas_call | solution.py:51
  46.9 3.2 %collective-permute-start.8 = (bf16[256,1024]{1,0:T(8,128)(2,1)}, bf16[256,1024]{1,0:T(8,128)(2,1)S(1)}, u32[]{:S(2)}, u32[]{:S(2)}) collective-permute-start(bf16[256,1024]{1,0:T(8,128)(2,1)} %get-tuple-element.73.refs_5_), channel_id=1, source_target_pairs={{0,1},{1,2},{4,5},{5,6},{8,9},{9,10},{12,13},{13,14},{16,17},{17,1... | collective-permute-start | bytes 1572872 | tf_op jit(solution)/shard_map/ppermute | solution.py:391
  50.0 1.5 %collective-permute-start.9 = (bf16[256,1024]{1,0:T(8,128)(2,1)S(1)}, bf16[256,1024]{1,0:T(8,128)(2,1)}, u32[]{:S(2)}, u32[]{:S(2)}) collective-permute-start(bf16[256,1024]{1,0:T(8,128)(2,1)S(1)} %get-tuple-element.74.refs_6_), channel_id=1, source_target_pairs={{3,2},{2,1},{7,6},{6,5},{11,10},{10,9},{15,14},{14,13},{19,18},{18... | collective-permute-start | bytes 1572872 | tf_op jit(solution)/shard_map/ppermute | solution.py:391
  51.5 3.3 %collective-permute-done.4.refs_2_.refs_3_ = bf16[256,1024]{1,0:T(8,128)(2,1)S(1)} collective-permute-done((bf16[256,1024]{1,0:T(8,128)(2,1)S(1)}, bf16[256,1024]{1,0:T(8,128)(2,1)S(1)}, u32[]{:S(2)}, u32[]{:S(2)}) %collective-permute-start.4) | collective-permute-done | bytes 524320 | tf_op jit(solution)/shard_map/ppermute | solution.py:391
  56.2 4.4 %collective-permute-start.6 = (bf16[256,1024]{1,0:T(8,128)(2,1)S(1)}, bf16[256,1024]{1,0:T(8,128)(2,1)S(1)}, u32[]{:S(2)}, u32[]{:S(2)}) collective-permute-start(bf16[256,1024]{1,0:T(8,128)(2,1)S(1)} %get-tuple-element.75.refs_6_), channel_id=1, source_target_pairs={{0,1},{1,2},{4,5},{5,6},{8,9},{9,10},{12,13},{13,14},{16,17},{17,1... | collective-permute-start | bytes 1572872 | tf_op jit(solution)/shard_map/ppermute | solution.py:391
  61.3 4.8 %collective-permute-done.8.refs_3_ = bf16[256,1024]{1,0:T(8,128)(2,1)S(1)} collective-permute-done((bf16[256,1024]{1,0:T(8,128)(2,1)}, bf16[256,1024]{1,0:T(8,128)(2,1)S(1)}, u32[]{:S(2)}, u32[]{:S(2)}) %collective-permute-start.8) | collective-permute-done | bytes 524320 | tf_op jit(solution)/shard_map/ppermute | solution.py:391
  66.1 2.5 %shard_map.75 = (bf16[256,1024]{1,0:T(8,128)(2,1)S(1)}, bf16[256,1024]{1,0:T(8,128)(2,1)S(1)}, bf16[256,1024]{1,0:T(8,128)(2,1)S(1)}) custom-call(s32[1]{0:T(128)} %bitcast.refs_0_, s32[1]{0:T(128)} %bitcast.1.refs_1_, s32[1]{0:T(128)} %bitcast.2.refs_2_, bf16[256,1024]{1,0:T(8,128)(2,1)S(1)} %collective-permute-done.8.refs_3_, ...), custom_call_target="tpu_custom_call" | custom-call | flops 67108864 | bytes 262144 | tf_op jit(solution)/shard_map/pallas_call | solution.py:51
  68.6 4.3 %collective-permute-start.12 = (bf16[256,1024]{1,0:T(8,128)(2,1)S(1)}, bf16[256,1024]{1,0:T(8,128)(2,1)S(1)}, u32[]{:S(2)}, u32[]{:S(2)}) collective-permute-start(bf16[256,1024]{1,0:T(8,128)(2,1)S(1)} %get-tuple-element.77.refs_6_), channel_id=1, source_target_pairs={{0,1},{1,2},{2,3},{4,5},{5,6},{6,7},{8,9},{9,10},{10,11},{12,13},{... | collective-permute-start | bytes 1572872 | tf_op jit(solution)/shard_map/ppermute | solution.py:391
  74.2 3.0 %collective-permute-done.6.refs_3_ = bf16[256,1024]{1,0:T(8,128)(2,1)S(1)} collective-permute-done((bf16[256,1024]{1,0:T(8,128)(2,1)S(1)}, bf16[256,1024]{1,0:T(8,128)(2,1)S(1)}, u32[]{:S(2)}, u32[]{:S(2)}) %collective-permute-start.6) | collective-permute-done | bytes 524320 | tf_op jit(solution)/shard_map/ppermute | solution.py:391
  77.3 1.4 %shard_map.76 = (bf16[256,1024]{1,0:T(8,128)(2,1)S(1)}, bf16[256,1024]{1,0:T(8,128)(2,1)S(1)}, bf16[256,1024]{1,0:T(8,128)(2,1)S(1)}) custom-call(s32[1]{0:T(128)} %bitcast.refs_0_, s32[1]{0:T(128)} %bitcast.1.refs_1_, s32[1]{0:T(128)} %bitcast.2.refs_2_, bf16[256,1024]{1,0:T(8,128)(2,1)S(1)} %collective-permute-done.6.refs_3_, ...), custom_call_target="tpu_custom_call" | custom-call | flops 67108864 | bytes 262144 | tf_op jit(solution)/shard_map/pallas_call | solution.py:51
  78.7 4.4 %collective-permute-start.10 = (bf16[256,1024]{1,0:T(8,128)(2,1)S(1)}, bf16[256,1024]{1,0:T(8,128)(2,1)S(1)}, u32[]{:S(2)}, u32[]{:S(2)}) collective-permute-start(bf16[256,1024]{1,0:T(8,128)(2,1)S(1)} %get-tuple-element.80), channel_id=1, source_target_pairs={{0,1},{1,2},{2,3},{4,5},{5,6},{6,7},{8,9},{9,10},{10,11},{12,13},{... | collective-permute-start | bytes 1572872 | tf_op jit(solution)/shard_map/ppermute | solution.py:391
  84.4 4.1 %collective-permute-done.12.up = bf16[256,1024]{1,0:T(8,128)(2,1)S(1)} collective-permute-done((bf16[256,1024]{1,0:T(8,128)(2,1)S(1)}, bf16[256,1024]{1,0:T(8,128)(2,1)S(1)}, u32[]{:S(2)}, u32[]{:S(2)}) %collective-permute-start.12) | collective-permute-done | bytes 524320 | tf_op jit(solution)/shard_map/ppermute | solution.py:391
  89.4 9.5 %collective-permute-done.10.up = bf16[256,1024]{1,0:T(8,128)(2,1)S(1)} collective-permute-done((bf16[256,1024]{1,0:T(8,128)(2,1)S(1)}, bf16[256,1024]{1,0:T(8,128)(2,1)S(1)}, u32[]{:S(2)}, u32[]{:S(2)}) %collective-permute-start.10) | collective-permute-done | bytes 524320 | tf_op jit(solution)/shard_map/ppermute | solution.py:391
  (21 shorter events, 9.8 us)
Async XLA Ops:
  8.9 15.2 %copy-start = (bf16[1024]{0:T(1024)(128)(2,1)S(1)}, bf16[1024]{0:T(1024)(128)(2,1)}, u32[]{:S(2)}) copy-start(bf16[1024]{0:T(1024)(128)(2,1)} %refs_2_.3) | copy-start | bytes 6148
  8.9 1.8 %collective-permute-start = (bf16[1296,128]{1,0:T(8,128)(2,1)S(1)}, bf16[1296,128]{1,0:T(8,128)(2,1)S(1)}, u32[]{:S(2)}, u32[]{:S(2)}) collective-permute-start(bf16[1296,128]{1,0:T(8,128)(2,1)S(1)} %get-tuple-element.44.mine), channel_id=1, source_target_pairs={{0,4},{4,0},{8,12},{12,8},{16,20},{20,16},{24,28},{28,24},{1,5},{5... | collective-permute-start | bytes 995336 | tf_op jit(solution)/shard_map/ppermute | solution.py:496
  10.7 6.3 %collective-permute-start.1 = (bf16[656,128]{1,0:T(8,128)(2,1)S(1)}, bf16[656,128]{1,0:T(8,128)(2,1)S(1)}, u32[]{:S(2)}, u32[]{:S(2)}) collective-permute-start(bf16[656,128]{1,0:T(8,128)(2,1)S(1)} %shard_map.65.mine), channel_id=1, source_target_pairs={{0,8},{4,20},{8,0},{12,28},{16,24},{20,4},{24,16},{28,12},{1,9},{5... | collective-permute-start | bytes 503816 | tf_op jit(solution)/shard_map/ppermute | solution.py:496
  17.1 5.5 %collective-permute-start.2 = (bf16[656,128]{1,0:T(8,128)(2,1)S(1)}, bf16[656,128]{1,0:T(8,128)(2,1)S(1)}, u32[]{:S(2)}, u32[]{:S(2)}) collective-permute-start(bf16[656,128]{1,0:T(8,128)(2,1)S(1)} %shard_map.66), channel_id=1, source_target_pairs={{0,16},{4,12},{8,24},{12,4},{16,0},{20,28},{24,8},{28,20},{1,17},{... | collective-permute-start | bytes 503816 | tf_op jit(solution)/shard_map/ppermute | solution.py:496
  22.6 1.5 %collective-permute-start.3 = (bf16[656,128]{1,0:T(8,128)(2,1)S(1)}, bf16[656,128]{1,0:T(8,128)(2,1)S(1)}, u32[]{:S(2)}, u32[]{:S(2)}) collective-permute-start(bf16[656,128]{1,0:T(8,128)(2,1)S(1)} %shard_map.69.refs_4_), channel_id=1, source_target_pairs={{0,4},{4,0},{8,12},{12,8},{16,20},{20,16},{24,28},{28,24},{1,5},{5... | collective-permute-start | bytes 503816 | tf_op jit(solution)/shard_map/ppermute | solution.py:496
  27.3 17.5 %collective-permute-start.5 = (bf16[256,1024]{1,0:T(8,128)(2,1)S(1)}, bf16[256,1024]{1,0:T(8,128)(2,1)S(1)}, u32[]{:S(2)}, u32[]{:S(2)}) collective-permute-start(bf16[256,1024]{1,0:T(8,128)(2,1)S(1)} %get-tuple-element.69.refs_13_), channel_id=1, source_target_pairs={{0,1},{3,2},{4,5},{7,6},{8,9},{11,10},{12,13},{15,14},{16,17},{19,... | collective-permute-start | bytes 1572872 | tf_op jit(solution)/shard_map/ppermute | solution.py:391
  34.5 20.3 %collective-permute-start.4 = (bf16[256,1024]{1,0:T(8,128)(2,1)S(1)}, bf16[256,1024]{1,0:T(8,128)(2,1)S(1)}, u32[]{:S(2)}, u32[]{:S(2)}) collective-permute-start(bf16[256,1024]{1,0:T(8,128)(2,1)S(1)} %get-tuple-element.70), channel_id=1, source_target_pairs={{0,1},{3,2},{4,5},{7,6},{8,9},{11,10},{12,13},{15,14},{16,17},{19,... | collective-permute-start | bytes 1572872 | tf_op jit(solution)/shard_map/ppermute | solution.py:391
  46.9 19.3 %collective-permute-start.8 = (bf16[256,1024]{1,0:T(8,128)(2,1)}, bf16[256,1024]{1,0:T(8,128)(2,1)S(1)}, u32[]{:S(2)}, u32[]{:S(2)}) collective-permute-start(bf16[256,1024]{1,0:T(8,128)(2,1)} %get-tuple-element.73.refs_5_), channel_id=1, source_target_pairs={{0,1},{1,2},{4,5},{5,6},{8,9},{9,10},{12,13},{13,14},{16,17},{17,1... | collective-permute-start | bytes 1572872 | tf_op jit(solution)/shard_map/ppermute | solution.py:391
  50.0 16.1 %collective-permute-start.9 = (bf16[256,1024]{1,0:T(8,128)(2,1)S(1)}, bf16[256,1024]{1,0:T(8,128)(2,1)}, u32[]{:S(2)}, u32[]{:S(2)}) collective-permute-start(bf16[256,1024]{1,0:T(8,128)(2,1)S(1)} %get-tuple-element.74.refs_6_), channel_id=1, source_target_pairs={{3,2},{2,1},{7,6},{6,5},{11,10},{10,9},{15,14},{14,13},{19,18},{18... | collective-permute-start | bytes 1572872 | tf_op jit(solution)/shard_map/ppermute | solution.py:391
  56.2 21.1 %collective-permute-start.6 = (bf16[256,1024]{1,0:T(8,128)(2,1)S(1)}, bf16[256,1024]{1,0:T(8,128)(2,1)S(1)}, u32[]{:S(2)}, u32[]{:S(2)}) collective-permute-start(bf16[256,1024]{1,0:T(8,128)(2,1)S(1)} %get-tuple-element.75.refs_6_), channel_id=1, source_target_pairs={{0,1},{1,2},{4,5},{5,6},{8,9},{9,10},{12,13},{13,14},{16,17},{17,1... | collective-permute-start | bytes 1572872 | tf_op jit(solution)/shard_map/ppermute | solution.py:391
  60.6 16.7 %collective-permute-start.7 = (bf16[256,1024]{1,0:T(8,128)(2,1)S(1)}, bf16[256,1024]{1,0:T(8,128)(2,1)S(1)}, u32[]{:S(2)}, u32[]{:S(2)}) collective-permute-start(bf16[256,1024]{1,0:T(8,128)(2,1)S(1)} %get-tuple-element.76.refs_7_), channel_id=1, source_target_pairs={{3,2},{2,1},{7,6},{6,5},{11,10},{10,9},{15,14},{14,13},{19,18},{18... | collective-permute-start | bytes 1572872 | tf_op jit(solution)/shard_map/ppermute | solution.py:391
  68.6 19.9 %collective-permute-start.12 = (bf16[256,1024]{1,0:T(8,128)(2,1)S(1)}, bf16[256,1024]{1,0:T(8,128)(2,1)S(1)}, u32[]{:S(2)}, u32[]{:S(2)}) collective-permute-start(bf16[256,1024]{1,0:T(8,128)(2,1)S(1)} %get-tuple-element.77.refs_6_), channel_id=1, source_target_pairs={{0,1},{1,2},{2,3},{4,5},{5,6},{6,7},{8,9},{9,10},{10,11},{12,13},{... | collective-permute-start | bytes 1572872 | tf_op jit(solution)/shard_map/ppermute | solution.py:391
  72.9 15.6 %collective-permute-start.13 = (bf16[256,1024]{1,0:T(8,128)(2,1)S(1)}, bf16[256,1024]{1,0:T(8,128)(2,1)S(1)}, u32[]{:S(2)}, u32[]{:S(2)}) collective-permute-start(bf16[256,1024]{1,0:T(8,128)(2,1)S(1)} %get-tuple-element.78.refs_7_), channel_id=1, source_target_pairs={{3,2},{2,1},{1,0},{7,6},{6,5},{5,4},{11,10},{10,9},{9,8},{15,14},{... | collective-permute-start | bytes 1572872 | tf_op jit(solution)/shard_map/ppermute | solution.py:391
  78.7 20.2 %collective-permute-start.10 = (bf16[256,1024]{1,0:T(8,128)(2,1)S(1)}, bf16[256,1024]{1,0:T(8,128)(2,1)S(1)}, u32[]{:S(2)}, u32[]{:S(2)}) collective-permute-start(bf16[256,1024]{1,0:T(8,128)(2,1)S(1)} %get-tuple-element.80), channel_id=1, source_target_pairs={{0,1},{1,2},{2,3},{4,5},{5,6},{6,7},{8,9},{9,10},{10,11},{12,13},{... | collective-permute-start | bytes 1572872 | tf_op jit(solution)/shard_map/ppermute | solution.py:391
  83.1 15.8 %collective-permute-start.11 = (bf16[256,1024]{1,0:T(8,128)(2,1)S(1)}, bf16[256,1024]{1,0:T(8,128)(2,1)S(1)}, u32[]{:S(2)}, u32[]{:S(2)}) collective-permute-start(bf16[256,1024]{1,0:T(8,128)(2,1)S(1)} %get-tuple-element.81), channel_id=1, source_target_pairs={{3,2},{2,1},{1,0},{7,6},{6,5},{5,4},{11,10},{10,9},{9,8},{15,14},{... | collective-permute-start | bytes 1572872 | tf_op jit(solution)/shard_map/ppermute | solution.py:391

commit v2 on v1

--- a/solution.py
+++ b/solution.py
@@ -11,10 +11,11 @@
 DV = 128
 ROLLS = F // 2
 FEATURES = 2 * F + (ROLLS - 1) * F + F
+WIDE = 256
 HALF_ROOT = 0.7071067811865476
 DEPTH_TILE = 1024
-AHEAD = 2
-PIECES = 1
+AHEAD = 3
+PIECES = 2
 VMEM_LIMIT = 24 * 1024 * 1024
 NT = (((1,), (1,)), ((), ()))
 f32 = jnp.float32
@@ -156,23 +157,22 @@
     )
 
 
-def local_kernel(start, q, k, v, numerators, denominators, features):
+def local_kernel(start, q, k, v, numerators, features):
     rows = q.shape[0]
+    half = rows // 2
     turned = q[...].astype(f32).T
-    for i in range(features.shape[0]):
-        blocks = feature_blocks(turned[(start + i) * F : (start + i + 1) * F], True)
-        features[i] = jnp.concatenate(blocks, axis=0).T.astype(bf16)
-    half = rows // 2
     lane = lax.broadcasted_iota(jnp.int32, q.shape, 1)
     row = lax.broadcasted_iota(jnp.int32, (half, half), 0)
     column = lax.broadcasted_iota(jnp.int32, (half, half), 1)
     queries = q[...]
     keys = k[...]
     ones = jnp.ones((rows, DV), bf16)
-    wide_lane = lax.broadcasted_iota(jnp.int32, (half, DV), 1)
-    sums = [jnp.zeros((half, DV), f32)] * 2
-    for i in range(numerators.shape[1] // DV):
+    tail_lane = lax.broadcasted_iota(jnp.int32, (half, WIDE - DV), 1) + DV
+    padding = jnp.zeros((WIDE - FEATURES, rows), f32)
+    for i in range(features.shape[0]):
         h = start + i
+        blocks = feature_blocks(turned[h * F : (h + 1) * F], True)
+        products = jnp.concatenate(blocks + [padding], axis=0).T
         mine = jnp.where(lane // F == h, queries, jnp.zeros_like(queries))
         values = jnp.concatenate([v[:, h * DV : (h + 1) * DV], ones], axis=1)
 
@@ -192,21 +192,20 @@
         lower = jnp.concatenate([weights(1, 0), weights(1, 1)], axis=1)
         lower = jnp.dot(lower, values, preferred_element_type=f32)
         for j, both in enumerate((upper, lower)):
-            numerators[j * half : (j + 1) * half, i * DV : (i + 1) * DV] = both[:, :DV].astype(bf16)
-            sums[j] = jnp.where(wide_lane == i, both[:, DV:], sums[j])
-    for j in range(2):
-        denominators[j * half : (j + 1) * half] = sums[j]
+            part = slice(j * half, (j + 1) * half)
+            numerators[part, i * DV : (i + 1) * DV] = both[:, :DV].astype(bf16)
+            high = both[:, DV:].astype(bf16).astype(f32)
+            tail = jnp.where(tail_lane == FEATURES, high, products[part, DV:])
+            tail = jnp.where(tail_lane == FEATURES + 1, both[:, DV:] - high, tail)
+            features[i, part, :DV] = products[part, :DV].astype(bf16)
+            features[i, part, DV:] = tail.astype(bf16)
 
 
 def local_attention(q, k, v, start, count):
     rows = q.shape[0]
     return call(
         functools.partial(local_kernel, start),
-        [
-            ((rows, count * DV), bf16, "hbm"),
-            ((rows, DV), f32, "hbm"),
-            ((count, rows, FEATURES), bf16, "hbm"),
-        ],
+        [((rows, count * DV), bf16, "hbm"), ((count, rows, WIDE), bf16, "hbm")],
         count * 4 * rows * rows * 2 * DV,
         vmem=[q, k, v],
     )
@@ -215,8 +214,8 @@
 def finish_kernel(begin, shards, rounds, parts, *refs):
     me, chunk, gain, *refs = refs
     received, (w, *refs) = refs[:rounds], refs[rounds:]
-    sources, (normalized, out) = refs[: 3 * parts], refs[-9:-7]
-    held_features, held_numerators, held_denominators, held_w, wide, products, sems = refs[-7:]
+    sources, (normalized, out) = refs[: 2 * parts], refs[-9:-7]
+    held_features, held_numerators, held_w, wide, products, squares, sems = refs[-7:]
     heads, rows, _ = held_features.shape
     split = heads // parts
     width = out.shape[1]
@@ -228,49 +227,47 @@
         early.append(pltpu.make_async_copy(source, target, sems.at[len(early)]))
 
     for i in range(parts):
-        numerators, denominators, features = sources[3 * i : 3 * i + 3]
+        numerators, features = sources[2 * i : 2 * i + 2]
         fetch(features.at[:, part, :], held_features.at[pl.ds(i * split, split)])
         fetch(numerators.at[part, :], held_numerators.at[i])
-        fetch(denominators.at[part, :], held_denominators.at[i])
-    late = []
-    for i in range(PIECES):
-        some = pl.ds(i * (w.shape[0] // PIECES), w.shape[0] // PIECES)
-        late.append(pltpu.make_async_copy(w.at[some, columns], held_w.at[some, :], sems.at[3 * parts + i]))
-    for copy in early + late:
+    late = pltpu.make_async_copy(w.at[:, columns], held_w, sems.at[2 * parts])
+    for copy in early + [late]:
         copy.start()
 
     sums, states = prefix_states(shards, me[0], heads, received)
     sums = jnp.concatenate([sums[:8], sums[8:, : FEATURES - 128]], axis=1)
     sums = jnp.concatenate([sums, jnp.zeros((DV - 8, FEATURES), f32)], axis=0).T
+    row = lax.broadcasted_iota(jnp.int32, (WIDE - FEATURES, 2 * DV), 0)
+    lane = lax.broadcasted_iota(jnp.int32, (WIDE - FEATURES, 2 * DV), 1)
+    below = jnp.where((row < 2) & (lane >= DV), 1.0, 0.0).astype(bf16)
     prefixes = []
     for h in range(heads):
         wide_sums = jnp.broadcast_to(sums[:, h : h + 1], (FEATURES, DV))
-        prefixes.append(jnp.concatenate([states(h), wide_sums], axis=1).astype(bf16))
+        above = jnp.concatenate([states(h), wide_sums], axis=1).astype(bf16)
+        prefixes.append(jnp.concatenate([above, below], axis=0))
     for copy in early:
         copy.wait()
     for h in range(heads):
         products[h] = jnp.dot(held_features[h], prefixes[h], preferred_element_type=f32)
-    spreads = []
     for h in range(heads):
         p, i = h // split, h % split
         numerator = products[h, :, :DV] + held_numerators[p, :, i * DV : (i + 1) * DV].astype(f32)
-        denominator = products[h, :, DV:] + held_denominators[p, :, i : i + 1]
-        products[h, :, :DV] = numerator / denominator
-    for h in range(heads):
-        ratio = products[h, :, :DV]
-        spreads.append(jnp.mean(ratio * ratio, axis=1, keepdims=True))
+        ratio = numerator / products[h, :, DV:]
+        products[h, :, :DV] = ratio
+        squares[h * rows : (h + 1) * rows] = (ratio * ratio).astype(bf16)
+    averaging = jnp.full((DV, DV), 1.0 / DV, bf16)
+    spread = jnp.dot(squares[...], averaging, preferred_element_type=f32)
     for h in range(heads):
         columns = slice(h * DV, (h + 1) * DV)
-        scaled = products[h, :, :DV] * lax.rsqrt(spreads[h] + 1e-06) * gain[columns].astype(f32).reshape(1, DV)
-        wide[:, columns] = scaled.astype(bf16)
+        scale = lax.rsqrt(spread[h * rows : (h + 1) * rows] + 1e-06) * gain[columns].astype(f32).reshape(1, DV)
+        wide[:, columns] = (products[h, :, :DV] * scale).astype(bf16)
     normalized[...] = wide[...]
-    for copy in late:
-        copy.wait()
+    late.wait()
     out[...] = jnp.dot(wide[...], held_w[...], preferred_element_type=f32).astype(bf16)
 
 
 def finish(shards, me, chunk, gain, w, local, received, begin, rows, width, after):
-    heads = sum(features.shape[0] for _, _, features in local)
+    heads = sum(features.shape[0] for _, features in local)
     parts = len(local)
     return call(
         functools.partial(finish_kernel, begin, shards, len(received), parts),
@@ -281,24 +278,23 @@
         hbm=[w, *[array for arrays in local for array in arrays]],
         loose=after,
         scratch_shapes=[
-            pltpu.VMEM((heads, rows, FEATURES), bf16),
+            pltpu.VMEM((heads, rows, WIDE), bf16),
             pltpu.VMEM((parts, rows, heads // parts * DV), bf16),
-            pltpu.VMEM((parts, rows, DV), f32),
             pltpu.VMEM((w.shape[0], width), bf16),
             pltpu.VMEM((rows, heads * DV), bf16),
             pltpu.VMEM((heads, rows, 2 * DV), f32),
-            pltpu.SemaphoreType.DMA((3 * parts + PIECES,)),
+            pltpu.VMEM((heads * rows, DV), bf16),
+            pltpu.SemaphoreType.DMA((2 * parts + 1,)),
         ],
     )
 
 
-def partials_kernel(*refs):
-    w, normalized, out = refs[:PIECES], refs[PIECES:-1], refs[-1]
+def partials_kernel(w, *refs):
+    *normalized, out = refs
     begin = 0
-    w = jnp.concatenate([piece[...] for piece in w], axis=0)
     for block in normalized:
         rows = block.shape[0]
-        out[0, begin : begin + rows] = jnp.dot(block[...], w, preferred_element_type=f32).astype(bf16)
+        out[0, begin : begin + rows] = jnp.dot(block[...], w[...], preferred_element_type=f32).astype(bf16)
         begin += rows
 
 
@@ -307,18 +303,17 @@
     tile = columns // count
     rows = sum(block.shape[0] for block in normalized)
     whole = lambda a: pl.BlockSpec(a.shape, lambda i: (0,) * a.ndim)
-    piece = lambda p: pl.BlockSpec((depth // PIECES, tile), lambda i: (p, i))
     return pl.pallas_call(
         partials_kernel,
         grid=(count,),
-        in_specs=[piece(p) for p in range(PIECES)] + [whole(block) for block in normalized],
+        in_specs=[pl.BlockSpec((depth, tile), lambda i: (0, i))] + [whole(block) for block in normalized],
         out_specs=pl.BlockSpec((1, rows, tile), lambda i: (i, 0, 0)),
         out_shape=pltpu.HBM((count, rows, tile), bf16),
         compiler_params=pltpu.CompilerParams(vmem_limit_bytes=VMEM_LIMIT),
         cost_estimate=pl.CostEstimate(
             flops=2 * rows * depth * columns, bytes_accessed=2 * depth * columns, transcendentals=0
         ),
-    )(*[in_hbm(w)] * PIECES, *[in_hbm(block) for block in normalized])
+    )(in_hbm(w), *[in_hbm(block) for block in normalized])
 
 
 def messages_kernel(begin, count, *refs):

time: 101 us -> 100 us (0.990)
  Pallas kernels: 38.8 us -> 37.6 us
    pallas_call x14, Pallas kernels: 30 us -> 28.9 us  [call(): pl.pallas_call(kernel, in_specs=[pl.BlockSpec(memory_space=pltpu.SMEM)] *...]
  transfers between devices with their start and end apart: 14 -> 14, of which waited for: 9 -> 9; matrix products, arithmetic and copies ran while one was open for 0% -> 0% of each run, Pallas kernels for 26% -> 25%
where the time goes in v2:
time: 100 us; the launch traced here: 99.4 us
  Pallas kernels  37.6 us (38%)
  starting transfers between devices  32.3 us (32%)
  waiting for transfers between devices  29.1 us (29%)
    pallas_call x14, Pallas kernels, call(): pl.pallas_call(kernel, in_specs=[pl.BlockSpec(memory_space=pltpu.SMEM)] *...  28.9 us
    ppermute x10, starting transfers between devices, send(): return lax.ppermute(block, 'tp', pairs)  26.7 us
    ppermute x10, waiting for transfers between devices, send(): return lax.ppermute(block, 'tp', pairs)  24.8 us
    pallas_call x1, Pallas kernels, partials(): pl.pallas_call(partials_kernel, grid=(count,), in_specs=[pl.BlockSpec((de...  8.75 us
    ppermute x4, starting transfers between devices, swap(): lax.ppermute(block, 'ctx', [(i, i ^ 1 << across[i]) for i in range(shards)])  5.63 us
    ppermute x4, waiting for transfers between devices, swap(): lax.ppermute(block, 'ctx', [(i, i ^ 1 << across[i]) for i in range(shards)])  4.26 us
  transfers between devices with their start and end apart: 14, of which 9 were waited for; matrix products, arithmetic and copies ran while one was open for 0% of the time, Pallas kernels for 25%

profile of v2, /device:TPU:0, one launch (start us, length us, event | category | flops | bytes accessed | tf_op | source)
XLA Modules:
  0.0 99.4 jit_solution(10465200313130296474)
XLA Ops:
  0.0 8.4 %shard_map.64 = (bf16[512,128]{1,0:T(8,128)(2,1)S(1)}, bf16[512,128]{1,0:T(8,128)(2,1)S(1)}, bf16[512,1024]{1,0:T(8,128)(2,1)S(1)}, bf16[1296,128]{1,0:T(8,128)(2,1)S(1)}) custom-call(bf16[512,4096]{1,0:T(8,128)(2,1)} %tokens.1, bf16[4096,128]{1,0:T(8,128)(2,1)} %wq.1, bf16[4096,128]{1,0:T(8,128)(2,1)} %wk.1, bf16[4096,1024]{1,0:T(8,128)(2,1)} %wv.1), custom_call_target="tpu_custom_call" | custom-call | flops 5368709120 | bytes 20971520 | tf_op jit(solution)/shard_map/pallas_call | solution.py:52
  10.3 2.9 %collective-permute-start.1 = (bf16[656,128]{1,0:T(8,128)(2,1)S(1)}, bf16[656,128]{1,0:T(8,128)(2,1)S(1)}, u32[]{:S(2)}, u32[]{:S(2)}) collective-permute-start(bf16[656,128]{1,0:T(8,128)(2,1)S(1)} %shard_map.65.mine), channel_id=1, source_target_pairs={{0,8},{4,20},{8,0},{12,28},{16,24},{20,4},{24,16},{28,12},{1,9},{5... | collective-permute-start | bytes 503816 | tf_op jit(solution)/shard_map/ppermute | solution.py:491
  13.2 2.5 %shard_map.67 = (bf16[512,512]{1,0:T(8,128)(2,1)}, bf16[4,512,256]{2,1,0:T(8,128)(2,1)}) custom-call(bf16[512,128]{1,0:T(8,128)(2,1)S(1)} %get-tuple-element.48.q, bf16[512,128]{1,0:T(8,128)(2,1)S(1)} %get-tuple-element.49.k, bf16[512,1024]{1,0:T(8,128)(2,1)S(1)} %get-tuple-element.50.v), custom_call_target="tpu_custom_call" | custom-call | flops 1073741824 | bytes 4194304 | tf_op jit(solution)/shard_map/pallas_call | solution.py:52
  16.6 2.1 %collective-permute-start.2 = (bf16[656,128]{1,0:T(8,128)(2,1)S(1)}, bf16[656,128]{1,0:T(8,128)(2,1)S(1)}, u32[]{:S(2)}, u32[]{:S(2)}) collective-permute-start(bf16[656,128]{1,0:T(8,128)(2,1)S(1)} %shard_map.66), channel_id=1, source_target_pairs={{0,16},{4,12},{8,24},{12,4},{16,0},{20,28},{24,8},{28,20},{1,17},{... | collective-permute-start | bytes 503816 | tf_op jit(solution)/shard_map/ppermute | solution.py:491
  18.8 2.5 %shard_map.68 = (bf16[512,512]{1,0:T(8,128)(2,1)}, bf16[4,512,256]{2,1,0:T(8,128)(2,1)}) custom-call(bf16[512,128]{1,0:T(8,128)(2,1)S(1)} %get-tuple-element.48.q, bf16[512,128]{1,0:T(8,128)(2,1)S(1)} %get-tuple-element.49.k, bf16[512,1024]{1,0:T(8,128)(2,1)S(1)} %get-tuple-element.50.v), custom_call_target="tpu_custom_call" | custom-call | flops 1073741824 | bytes 4194304 | tf_op jit(solution)/shard_map/pallas_call | solution.py:52
  22.3 1.4 %collective-permute-done.3.refs_5_ = bf16[656,128]{1,0:T(8,128)(2,1)S(1)} collective-permute-done((bf16[656,128]{1,0:T(8,128)(2,1)S(1)}, bf16[656,128]{1,0:T(8,128)(2,1)S(1)}, u32[]{:S(2)}, u32[]{:S(2)}) %collective-permute-start.3) | collective-permute-done | bytes 167968 | tf_op jit(solution)/shard_map/ppermute | solution.py:491
  23.6 3.1 %shard_map.70 = (bf16[256,1024]{1,0:T(8,128)(2,1)}, bf16[256,1024]{1,0:T(8,128)(2,1)S(1)}) custom-call(s32[1]{0:T(128)} %bitcast.5.me.refs_0_, s32[1]{0:T(128)} %bitcast.6.refs_1_, bf16[1024]{0:T(1024)(128)(2,1)S(1)} %copy-done, bf16[1296,128]{1,0:T(8,128)(2,1)S(1)} %collective-permute-done.other.refs_3_, bf16[656,128]{1,0:T(8,128)(2,1)S(1)} %shard_map.69.refs_4_, ...), custom_call_target="tpu_custom_call" | custom-call | flops 805306368 | bytes 3145728 | tf_op jit(solution)/shard_map/pallas_call | solution.py:52
  26.7 4.0 %collective-permute-start.5 = (bf16[256,1024]{1,0:T(8,128)(2,1)S(1)}, bf16[256,1024]{1,0:T(8,128)(2,1)S(1)}, u32[]{:S(2)}, u32[]{:S(2)}) collective-permute-start(bf16[256,1024]{1,0:T(8,128)(2,1)S(1)} %get-tuple-element.59.refs_11_), channel_id=1, source_target_pairs={{0,1},{3,2},{4,5},{7,6},{8,9},{11,10},{12,13},{15,14},{16,17},{19,... | collective-permute-start | bytes 1572872 | tf_op jit(solution)/shard_map/ppermute | solution.py:386
  30.7 3.0 %shard_map.71 = (bf16[256,1024]{1,0:T(8,128)(2,1)}, bf16[256,1024]{1,0:T(8,128)(2,1)S(1)}) custom-call(s32[1]{0:T(128)} %bitcast.5.me.refs_0_, s32[1]{0:T(128)} %bitcast.6.refs_1_, bf16[1024]{0:T(1024)(128)(2,1)S(1)} %copy-done, bf16[1296,128]{1,0:T(8,128)(2,1)S(1)} %collective-permute-done.other.refs_3_, bf16[656,128]{1,0:T(8,128)(2,1)S(1)} %shard_map.69.refs_4_, ...), custom_call_target="tpu_custom_call" | custom-call | flops 805306368 | bytes 3145728 | tf_op jit(solution)/shard_map/pallas_call | solution.py:52
  33.8 1.5 %collective-permute-start.4 = (bf16[256,1024]{1,0:T(8,128)(2,1)S(1)}, bf16[256,1024]{1,0:T(8,128)(2,1)S(1)}, u32[]{:S(2)}, u32[]{:S(2)}) collective-permute-start(bf16[256,1024]{1,0:T(8,128)(2,1)S(1)} %get-tuple-element.60), channel_id=1, source_target_pairs={{0,1},{3,2},{4,5},{7,6},{8,9},{11,10},{12,13},{15,14},{16,17},{19,... | collective-permute-start | bytes 1572872 | tf_op jit(solution)/shard_map/ppermute | solution.py:386
  35.3 8.8 %shard_map.72.refs_4_.refs_5_ = bf16[4,512,1024]{2,1,0:T(8,128)(2,1)} custom-call(bf16[1024,4096]{1,0:T(8,128)(2,1)} %w.1, bf16[256,1024]{1,0:T(8,128)(2,1)} %get-tuple-element.61.refs_0_, bf16[256,1024]{1,0:T(8,128)(2,1)} %get-tuple-element.62.refs_1_), custom_call_target="tpu_custom_call" | custom-call | flops 4294967296 | bytes 8388608 | tf_op jit(solution)/shard_map/pallas_call | solution.py:306
  44.1 2.0 %shard_map.73 = (bf16[256,1024]{1,0:T(8,128)(2,1)}, bf16[256,1024]{1,0:T(8,128)(2,1)S(1)}) custom-call(s32[1]{0:T(128)} %bitcast.3.refs_0_, s32[1]{0:T(128)} %bitcast.4.refs_1_, bf16[256,1024]{1,0:T(8,128)(2,1)S(1)} %collective-permute-done.5.refs_2_.refs_3_, bf16[256,1024]{1,0:T(8,128)(2,1)S(1)} %collective-permute-done.5.refs_2_.refs_3_, ...), custom_call_target="tpu_custom_call" | custom-call | flops 67108864 | bytes 262144 | tf_op jit(solution)/shard_map/pallas_call | solution.py:52
  46.1 3.3 %collective-permute-start.8 = (bf16[256,1024]{1,0:T(8,128)(2,1)}, bf16[256,1024]{1,0:T(8,128)(2,1)S(1)}, u32[]{:S(2)}, u32[]{:S(2)}) collective-permute-start(bf16[256,1024]{1,0:T(8,128)(2,1)} %get-tuple-element.63.refs_5_), channel_id=1, source_target_pairs={{0,1},{1,2},{4,5},{5,6},{8,9},{9,10},{12,13},{13,14},{16,17},{17,1... | collective-permute-start | bytes 1572872 | tf_op jit(solution)/shard_map/ppermute | solution.py:386
  49.4 1.5 %collective-permute-start.9 = (bf16[256,1024]{1,0:T(8,128)(2,1)S(1)}, bf16[256,1024]{1,0:T(8,128)(2,1)}, u32[]{:S(2)}, u32[]{:S(2)}) collective-permute-start(bf16[256,1024]{1,0:T(8,128)(2,1)S(1)} %get-tuple-element.64.refs_6_), channel_id=1, source_target_pairs={{3,2},{2,1},{7,6},{6,5},{11,10},{10,9},{15,14},{14,13},{19,18},{18... | collective-permute-start | bytes 1572872 | tf_op jit(solution)/shard_map/ppermute | solution.py:386
  50.9 3.3 %collective-permute-done.4.refs_2_.refs_3_ = bf16[256,1024]{1,0:T(8,128)(2,1)S(1)} collective-permute-done((bf16[256,1024]{1,0:T(8,128)(2,1)S(1)}, bf16[256,1024]{1,0:T(8,128)(2,1)S(1)}, u32[]{:S(2)}, u32[]{:S(2)}) %collective-permute-start.4) | collective-permute-done | bytes 524320 | tf_op jit(solution)/shard_map/ppermute | solution.py:386
  55.5 4.4 %collective-permute-start.6 = (bf16[256,1024]{1,0:T(8,128)(2,1)S(1)}, bf16[256,1024]{1,0:T(8,128)(2,1)S(1)}, u32[]{:S(2)}, u32[]{:S(2)}) collective-permute-start(bf16[256,1024]{1,0:T(8,128)(2,1)S(1)} %get-tuple-element.65.refs_6_), channel_id=1, source_target_pairs={{0,1},{1,2},{4,5},{5,6},{8,9},{9,10},{12,13},{13,14},{16,17},{17,1... | collective-permute-start | bytes 1572872 | tf_op jit(solution)/shard_map/ppermute | solution.py:386
  60.7 4.9 %collective-permute-done.8.refs_3_ = bf16[256,1024]{1,0:T(8,128)(2,1)S(1)} collective-permute-done((bf16[256,1024]{1,0:T(8,128)(2,1)}, bf16[256,1024]{1,0:T(8,128)(2,1)S(1)}, u32[]{:S(2)}, u32[]{:S(2)}) %collective-permute-start.8) | collective-permute-done | bytes 524320 | tf_op jit(solution)/shard_map/ppermute | solution.py:386
  65.5 2.5 %shard_map.75 = (bf16[256,1024]{1,0:T(8,128)(2,1)S(1)}, bf16[256,1024]{1,0:T(8,128)(2,1)S(1)}, bf16[256,1024]{1,0:T(8,128)(2,1)S(1)}) custom-call(s32[1]{0:T(128)} %bitcast.refs_0_, s32[1]{0:T(128)} %bitcast.1.refs_1_, s32[1]{0:T(128)} %bitcast.2.refs_2_, bf16[256,1024]{1,0:T(8,128)(2,1)S(1)} %collective-permute-done.8.refs_3_, ...), custom_call_target="tpu_custom_call" | custom-call | flops 67108864 | bytes 262144 | tf_op jit(solution)/shard_map/pallas_call | solution.py:52
  68.0 4.3 %collective-permute-start.12 = (bf16[256,1024]{1,0:T(8,128)(2,1)S(1)}, bf16[256,1024]{1,0:T(8,128)(2,1)S(1)}, u32[]{:S(2)}, u32[]{:S(2)}) collective-permute-start(bf16[256,1024]{1,0:T(8,128)(2,1)S(1)} %get-tuple-element.67.refs_6_), channel_id=1, source_target_pairs={{0,1},{1,2},{2,3},{4,5},{5,6},{6,7},{8,9},{9,10},{10,11},{12,13},{... | collective-permute-start | bytes 1572872 | tf_op jit(solution)/shard_map/ppermute | solution.py:386
  73.6 3.0 %collective-permute-done.6.refs_3_ = bf16[256,1024]{1,0:T(8,128)(2,1)S(1)} collective-permute-done((bf16[256,1024]{1,0:T(8,128)(2,1)S(1)}, bf16[256,1024]{1,0:T(8,128)(2,1)S(1)}, u32[]{:S(2)}, u32[]{:S(2)}) %collective-permute-start.6) | collective-permute-done | bytes 524320 | tf_op jit(solution)/shard_map/ppermute | solution.py:386
  76.7 1.4 %shard_map.76 = (bf16[256,1024]{1,0:T(8,128)(2,1)S(1)}, bf16[256,1024]{1,0:T(8,128)(2,1)S(1)}, bf16[256,1024]{1,0:T(8,128)(2,1)S(1)}) custom-call(s32[1]{0:T(128)} %bitcast.refs_0_, s32[1]{0:T(128)} %bitcast.1.refs_1_, s32[1]{0:T(128)} %bitcast.2.refs_2_, bf16[256,1024]{1,0:T(8,128)(2,1)S(1)} %collective-permute-done.6.refs_3_, ...), custom_call_target="tpu_custom_call" | custom-call | flops 67108864 | bytes 262144 | tf_op jit(solution)/shard_map/pallas_call | solution.py:52
  78.1 4.4 %collective-permute-start.10 = (bf16[256,1024]{1,0:T(8,128)(2,1)S(1)}, bf16[256,1024]{1,0:T(8,128)(2,1)S(1)}, u32[]{:S(2)}, u32[]{:S(2)}) collective-permute-start(bf16[256,1024]{1,0:T(8,128)(2,1)S(1)} %get-tuple-element.70), channel_id=1, source_target_pairs={{0,1},{1,2},{2,3},{4,5},{5,6},{6,7},{8,9},{9,10},{10,11},{12,13},{... | collective-permute-start | bytes 1572872 | tf_op jit(solution)/shard_map/ppermute | solution.py:386
  83.8 4.1 %collective-permute-done.12.up = bf16[256,1024]{1,0:T(8,128)(2,1)S(1)} collective-permute-done((bf16[256,1024]{1,0:T(8,128)(2,1)S(1)}, bf16[256,1024]{1,0:T(8,128)(2,1)S(1)}, u32[]{:S(2)}, u32[]{:S(2)}) %collective-permute-start.12) | collective-permute-done | bytes 524320 | tf_op jit(solution)/shard_map/ppermute | solution.py:386
  88.8 9.5 %collective-permute-done.10.up = bf16[256,1024]{1,0:T(8,128)(2,1)S(1)} collective-permute-done((bf16[256,1024]{1,0:T(8,128)(2,1)S(1)}, bf16[256,1024]{1,0:T(8,128)(2,1)S(1)}, u32[]{:S(2)}, u32[]{:S(2)}) %collective-permute-start.10) | collective-permute-done | bytes 524320 | tf_op jit(solution)/shard_map/ppermute | solution.py:386
  (21 shorter events, 10.2 us)
Async XLA Ops:
  8.4 15.2 %copy-start = (bf16[1024]{0:T(1024)(128)(2,1)S(1)}, bf16[1024]{0:T(1024)(128)(2,1)}, u32[]{:S(2)}) copy-start(bf16[1024]{0:T(1024)(128)(2,1)} %refs_2_.3) | copy-start | bytes 6148
  8.4 1.8 %collective-permute-start = (bf16[1296,128]{1,0:T(8,128)(2,1)S(1)}, bf16[1296,128]{1,0:T(8,128)(2,1)S(1)}, u32[]{:S(2)}, u32[]{:S(2)}) collective-permute-start(bf16[1296,128]{1,0:T(8,128)(2,1)S(1)} %get-tuple-element.39.mine), channel_id=1, source_target_pairs={{0,4},{4,0},{8,12},{12,8},{16,20},{20,16},{24,28},{28,24},{1,5},{5... | collective-permute-start | bytes 995336 | tf_op jit(solution)/shard_map/ppermute | solution.py:491
  10.3 6.3 %collective-permute-start.1 = (bf16[656,128]{1,0:T(8,128)(2,1)S(1)}, bf16[656,128]{1,0:T(8,128)(2,1)S(1)}, u32[]{:S(2)}, u32[]{:S(2)}) collective-permute-start(bf16[656,128]{1,0:T(8,128)(2,1)S(1)} %shard_map.65.mine), channel_id=1, source_target_pairs={{0,8},{4,20},{8,0},{12,28},{16,24},{20,4},{24,16},{28,12},{1,9},{5... | collective-permute-start | bytes 503816 | tf_op jit(solution)/shard_map/ppermute | solution.py:491
  16.6 5.5 %collective-permute-start.2 = (bf16[656,128]{1,0:T(8,128)(2,1)S(1)}, bf16[656,128]{1,0:T(8,128)(2,1)S(1)}, u32[]{:S(2)}, u32[]{:S(2)}) collective-permute-start(bf16[656,128]{1,0:T(8,128)(2,1)S(1)} %shard_map.66), channel_id=1, source_target_pairs={{0,16},{4,12},{8,24},{12,4},{16,0},{20,28},{24,8},{28,20},{1,17},{... | collective-permute-start | bytes 503816 | tf_op jit(solution)/shard_map/ppermute | solution.py:491
  22.2 1.5 %collective-permute-start.3 = (bf16[656,128]{1,0:T(8,128)(2,1)S(1)}, bf16[656,128]{1,0:T(8,128)(2,1)S(1)}, u32[]{:S(2)}, u32[]{:S(2)}) collective-permute-start(bf16[656,128]{1,0:T(8,128)(2,1)S(1)} %shard_map.69.refs_4_), channel_id=1, source_target_pairs={{0,4},{4,0},{8,12},{12,8},{16,20},{20,16},{24,28},{28,24},{1,5},{5... | collective-permute-start | bytes 503816 | tf_op jit(solution)/shard_map/ppermute | solution.py:491
  26.7 17.4 %collective-permute-start.5 = (bf16[256,1024]{1,0:T(8,128)(2,1)S(1)}, bf16[256,1024]{1,0:T(8,128)(2,1)S(1)}, u32[]{:S(2)}, u32[]{:S(2)}) collective-permute-start(bf16[256,1024]{1,0:T(8,128)(2,1)S(1)} %get-tuple-element.59.refs_11_), channel_id=1, source_target_pairs={{0,1},{3,2},{4,5},{7,6},{8,9},{11,10},{12,13},{15,14},{16,17},{19,... | collective-permute-start | bytes 1572872 | tf_op jit(solution)/shard_map/ppermute | solution.py:386
  33.8 20.4 %collective-permute-start.4 = (bf16[256,1024]{1,0:T(8,128)(2,1)S(1)}, bf16[256,1024]{1,0:T(8,128)(2,1)S(1)}, u32[]{:S(2)}, u32[]{:S(2)}) collective-permute-start(bf16[256,1024]{1,0:T(8,128)(2,1)S(1)} %get-tuple-element.60), channel_id=1, source_target_pairs={{0,1},{3,2},{4,5},{7,6},{8,9},{11,10},{12,13},{15,14},{16,17},{19,... | collective-permute-start | bytes 1572872 | tf_op jit(solution)/shard_map/ppermute | solution.py:386
  46.1 19.5 %collective-permute-start.8 = (bf16[256,1024]{1,0:T(8,128)(2,1)}, bf16[256,1024]{1,0:T(8,128)(2,1)S(1)}, u32[]{:S(2)}, u32[]{:S(2)}) collective-permute-start(bf16[256,1024]{1,0:T(8,128)(2,1)} %get-tuple-element.63.refs_5_), channel_id=1, source_target_pairs={{0,1},{1,2},{4,5},{5,6},{8,9},{9,10},{12,13},{13,14},{16,17},{17,1... | collective-permute-start | bytes 1572872 | tf_op jit(solution)/shard_map/ppermute | solution.py:386
  49.4 16.1 %collective-permute-start.9 = (bf16[256,1024]{1,0:T(8,128)(2,1)S(1)}, bf16[256,1024]{1,0:T(8,128)(2,1)}, u32[]{:S(2)}, u32[]{:S(2)}) collective-permute-start(bf16[256,1024]{1,0:T(8,128)(2,1)S(1)} %get-tuple-element.64.refs_6_), channel_id=1, source_target_pairs={{3,2},{2,1},{7,6},{6,5},{11,10},{10,9},{15,14},{14,13},{19,18},{18... | collective-permute-start | bytes 1572872 | tf_op jit(solution)/shard_map/ppermute | solution.py:386
  55.5 21.1 %collective-permute-start.6 = (bf16[256,1024]{1,0:T(8,128)(2,1)S(1)}, bf16[256,1024]{1,0:T(8,128)(2,1)S(1)}, u32[]{:S(2)}, u32[]{:S(2)}) collective-permute-start(bf16[256,1024]{1,0:T(8,128)(2,1)S(1)} %get-tuple-element.65.refs_6_), channel_id=1, source_target_pairs={{0,1},{1,2},{4,5},{5,6},{8,9},{9,10},{12,13},{13,14},{16,17},{17,1... | collective-permute-start | bytes 1572872 | tf_op jit(solution)/shard_map/ppermute | solution.py:386
  60.0 16.7 %collective-permute-start.7 = (bf16[256,1024]{1,0:T(8,128)(2,1)S(1)}, bf16[256,1024]{1,0:T(8,128)(2,1)S(1)}, u32[]{:S(2)}, u32[]{:S(2)}) collective-permute-start(bf16[256,1024]{1,0:T(8,128)(2,1)S(1)} %get-tuple-element.66.refs_7_), channel_id=1, source_target_pairs={{3,2},{2,1},{7,6},{6,5},{11,10},{10,9},{15,14},{14,13},{19,18},{18... | collective-permute-start | bytes 1572872 | tf_op jit(solution)/shard_map/ppermute | solution.py:386
  68.0 19.9 %collective-permute-start.12 = (bf16[256,1024]{1,0:T(8,128)(2,1)S(1)}, bf16[256,1024]{1,0:T(8,128)(2,1)S(1)}, u32[]{:S(2)}, u32[]{:S(2)}) collective-permute-start(bf16[256,1024]{1,0:T(8,128)(2,1)S(1)} %get-tuple-element.67.refs_6_), channel_id=1, source_target_pairs={{0,1},{1,2},{2,3},{4,5},{5,6},{6,7},{8,9},{9,10},{10,11},{12,13},{... | collective-permute-start | bytes 1572872 | tf_op jit(solution)/shard_map/ppermute | solution.py:386
  72.3 15.6 %collective-permute-start.13 = (bf16[256,1024]{1,0:T(8,128)(2,1)S(1)}, bf16[256,1024]{1,0:T(8,128)(2,1)S(1)}, u32[]{:S(2)}, u32[]{:S(2)}) collective-permute-start(bf16[256,1024]{1,0:T(8,128)(2,1)S(1)} %get-tuple-element.68.refs_7_), channel_id=1, source_target_pairs={{3,2},{2,1},{1,0},{7,6},{6,5},{5,4},{11,10},{10,9},{9,8},{15,14},{... | collective-permute-start | bytes 1572872 | tf_op jit(solution)/shard_map/ppermute | solution.py:386
  78.1 20.2 %collective-permute-start.10 = (bf16[256,1024]{1,0:T(8,128)(2,1)S(1)}, bf16[256,1024]{1,0:T(8,128)(2,1)S(1)}, u32[]{:S(2)}, u32[]{:S(2)}) collective-permute-start(bf16[256,1024]{1,0:T(8,128)(2,1)S(1)} %get-tuple-element.70), channel_id=1, source_target_pairs={{0,1},{1,2},{2,3},{4,5},{5,6},{6,7},{8,9},{9,10},{10,11},{12,13},{... | collective-permute-start | bytes 1572872 | tf_op jit(solution)/shard_map/ppermute | solution.py:386
  82.5 15.8 %collective-permute-start.11 = (bf16[256,1024]{1,0:T(8,128)(2,1)S(1)}, bf16[256,1024]{1,0:T(8,128)(2,1)S(1)}, u32[]{:S(2)}, u32[]{:S(2)}) collective-permute-start(bf16[256,1024]{1,0:T(8,128)(2,1)S(1)} %get-tuple-element.71), channel_id=1, source_target_pairs={{3,2},{2,1},{1,0},{7,6},{6,5},{5,4},{11,10},{10,9},{9,8},{15,14},{... | collective-permute-start | bytes 1572872 | tf_op jit(solution)/shard_map/ppermute | solution.py:386

commit v3 on v2

--- a/solution.py
+++ b/solution.py
@@ -261,9 +261,11 @@
         columns = slice(h * DV, (h + 1) * DV)
         scale = lax.rsqrt(spread[h * rows : (h + 1) * rows] + 1e-06) * gain[columns].astype(f32).reshape(1, DV)
         wide[:, columns] = (products[h, :, :DV] * scale).astype(bf16)
-    normalized[...] = wide[...]
+    aside = pltpu.make_async_copy(wide, normalized, sems.at[2 * parts + 1])
+    aside.start()
     late.wait()
     out[...] = jnp.dot(wide[...], held_w[...], preferred_element_type=f32).astype(bf16)
+    aside.wait()
 
 
 def finish(shards, me, chunk, gain, w, local, received, begin, rows, width, after):
@@ -271,7 +273,7 @@
     parts = len(local)
     return call(
         functools.partial(finish_kernel, begin, shards, len(received), parts),
-        [((rows, heads * DV), bf16, "hbm"), ((rows, width), bf16, "free")],
+        [((rows, heads * DV), bf16, "raw"), ((rows, width), bf16, "free")],
         2 * heads * rows * (256 * 256 + DV * width),
         smem=[me, chunk],
         free=[gain, *received],
@@ -284,7 +286,7 @@
             pltpu.VMEM((rows, heads * DV), bf16),
             pltpu.VMEM((heads, rows, 2 * DV), f32),
             pltpu.VMEM((heads * rows, DV), bf16),
-            pltpu.SemaphoreType.DMA((2 * parts + 1,)),
+            pltpu.SemaphoreType.DMA((2 * parts + 2,)),
         ],
     )
 
@@ -517,7 +519,7 @@
     def begin_block(begin, size, chunk, after):
         return finish(shards, me, chunk, norm_gain, out_weight, local, received, begin, size, width, after)
 
-    return reduced(begin_block, out_weight, rows, [0, rows // 2, rows])
+    return reduced(begin_block, out_weight, rows, [0, rows * 17 // 512 * 16, rows])
 
 
 def solution(mesh):

time: 100 us -> 99.9 us (level)
  no operation moved by 1% of the time
where the time goes in v3:
time: 99.9 us; the launch traced here: 99.4 us
  Pallas kernels  37.5 us (38%)
  starting transfers between devices  33.2 us (33%)
  waiting for transfers between devices  28.4 us (28%)
    pallas_call x14, Pallas kernels, call(): pl.pallas_call(kernel, in_specs=[pl.BlockSpec(memory_space=pltpu.SMEM)] *...  28.8 us
    ppermute x10, starting transfers between devices, send(): return lax.ppermute(block, 'tp', pairs)  27.5 us
    ppermute x10, waiting for transfers between devices, send(): return lax.ppermute(block, 'tp', pairs)  24.1 us
    pallas_call x1, Pallas kernels, partials(): pl.pallas_call(partials_kernel, grid=(count,), in_specs=[pl.BlockSpec((de...  8.73 us
    ppermute x4, starting transfers between devices, swap(): lax.ppermute(block, 'ctx', [(i, i ^ 1 << across[i]) for i in range(shards)])  5.63 us
    ppermute x4, waiting for transfers between devices, swap(): lax.ppermute(block, 'ctx', [(i, i ^ 1 << across[i]) for i in range(shards)])  4.27 us
  transfers between devices with their start and end apart: 14, of which 9 were waited for; matrix products, arithmetic and copies ran while one was open for 0% of the time, Pallas kernels for 25%

profile of v3, /device:TPU:0, one launch (start us, length us, event | category | flops | bytes accessed | tf_op | source)
XLA Modules:
  0.0 99.4 jit_solution(7982987802305952236)
XLA Ops:
  0.0 8.4 %shard_map.64 = (bf16[512,128]{1,0:T(8,128)(2,1)S(1)}, bf16[512,128]{1,0:T(8,128)(2,1)S(1)}, bf16[512,1024]{1,0:T(8,128)(2,1)S(1)}, bf16[1296,128]{1,0:T(8,128)(2,1)S(1)}) custom-call(bf16[512,4096]{1,0:T(8,128)(2,1)} %tokens.1, bf16[4096,128]{1,0:T(8,128)(2,1)} %wq.1, bf16[4096,128]{1,0:T(8,128)(2,1)} %wk.1, bf16[4096,1024]{1,0:T(8,128)(2,1)} %wv.1), custom_call_target="tpu_custom_call" | custom-call | flops 5368709120 | bytes 20971520 | tf_op jit(solution)/shard_map/pallas_call | solution.py:52
  10.3 2.9 %collective-permute-start.1 = (bf16[656,128]{1,0:T(8,128)(2,1)S(1)}, bf16[656,128]{1,0:T(8,128)(2,1)S(1)}, u32[]{:S(2)}, u32[]{:S(2)}) collective-permute-start(bf16[656,128]{1,0:T(8,128)(2,1)S(1)} %shard_map.65.mine), channel_id=1, source_target_pairs={{0,8},{4,20},{8,0},{12,28},{16,24},{20,4},{24,16},{28,12},{1,9},{5... | collective-permute-start | bytes 503816 | tf_op jit(solution)/shard_map/ppermute | solution.py:493
  13.2 2.5 %shard_map.67 = (bf16[512,512]{1,0:T(8,128)(2,1)}, bf16[4,512,256]{2,1,0:T(8,128)(2,1)}) custom-call(bf16[512,128]{1,0:T(8,128)(2,1)S(1)} %get-tuple-element.48.q, bf16[512,128]{1,0:T(8,128)(2,1)S(1)} %get-tuple-element.49.k, bf16[512,1024]{1,0:T(8,128)(2,1)S(1)} %get-tuple-element.50.v), custom_call_target="tpu_custom_call" | custom-call | flops 1073741824 | bytes 4194304 | tf_op jit(solution)/shard_map/pallas_call | solution.py:52
  16.6 2.1 %collective-permute-start.2 = (bf16[656,128]{1,0:T(8,128)(2,1)S(1)}, bf16[656,128]{1,0:T(8,128)(2,1)S(1)}, u32[]{:S(2)}, u32[]{:S(2)}) collective-permute-start(bf16[656,128]{1,0:T(8,128)(2,1)S(1)} %shard_map.66), channel_id=1, source_target_pairs={{0,16},{4,12},{8,24},{12,4},{16,0},{20,28},{24,8},{28,20},{1,17},{... | collective-permute-start | bytes 503816 | tf_op jit(solution)/shard_map/ppermute | solution.py:493
  18.8 2.5 %shard_map.68 = (bf16[512,512]{1,0:T(8,128)(2,1)}, bf16[4,512,256]{2,1,0:T(8,128)(2,1)}) custom-call(bf16[512,128]{1,0:T(8,128)(2,1)S(1)} %get-tuple-element.48.q, bf16[512,128]{1,0:T(8,128)(2,1)S(1)} %get-tuple-element.49.k, bf16[512,1024]{1,0:T(8,128)(2,1)S(1)} %get-tuple-element.50.v), custom_call_target="tpu_custom_call" | custom-call | flops 1073741824 | bytes 4194304 | tf_op jit(solution)/shard_map/pallas_call | solution.py:52
  23.6 3.0 %shard_map.70 = (bf16[272,1024]{1,0:T(8,128)(2,1)}, bf16[272,1024]{1,0:T(8,128)(2,1)S(1)}) custom-call(s32[1]{0:T(128)} %bitcast.5.me.refs_0_, s32[1]{0:T(128)} %bitcast.6.refs_1_, bf16[1024]{0:T(1024)(128)(2,1)S(1)} %copy-done, bf16[1296,128]{1,0:T(8,128)(2,1)S(1)} %collective-permute-done.other.refs_3_, bf16[656,128]{1,0:T(8,128)(2,1)S(1)} %shard_map.69.refs_4_, ...), custom_call_target="tpu_custom_call" | custom-call | flops 855638016 | bytes 3342336 | tf_op jit(solution)/shard_map/pallas_call | solution.py:52
  26.7 4.0 %collective-permute-start.5 = (bf16[272,1024]{1,0:T(8,128)(2,1)S(1)}, bf16[272,1024]{1,0:T(8,128)(2,1)S(1)}, u32[]{:S(2)}, u32[]{:S(2)}) collective-permute-start(bf16[272,1024]{1,0:T(8,128)(2,1)S(1)} %get-tuple-element.59.refs_11_), channel_id=1, source_target_pairs={{0,1},{3,2},{4,5},{7,6},{8,9},{11,10},{12,13},{15,14},{16,17},{19,... | collective-permute-start | bytes 1671176 | tf_op jit(solution)/shard_map/ppermute | solution.py:388
  30.7 3.0 %shard_map.71 = (bf16[240,1024]{1,0:T(8,128)(2,1)}, bf16[240,1024]{1,0:T(8,128)(2,1)S(1)}) custom-call(s32[1]{0:T(128)} %bitcast.5.me.refs_0_, s32[1]{0:T(128)} %bitcast.6.refs_1_, bf16[1024]{0:T(1024)(128)(2,1)S(1)} %copy-done, bf16[1296,128]{1,0:T(8,128)(2,1)S(1)} %collective-permute-done.other.refs_3_, bf16[656,128]{1,0:T(8,128)(2,1)S(1)} %shard_map.69.refs_4_, ...), custom_call_target="tpu_custom_call" | custom-call | flops 754974720 | bytes 2949120 | tf_op jit(solution)/shard_map/pallas_call | solution.py:52
  33.7 1.5 %collective-permute-start.4 = (bf16[240,1024]{1,0:T(8,128)(2,1)S(1)}, bf16[240,1024]{1,0:T(8,128)(2,1)S(1)}, u32[]{:S(2)}, u32[]{:S(2)}) collective-permute-start(bf16[240,1024]{1,0:T(8,128)(2,1)S(1)} %get-tuple-element.60), channel_id=1, source_target_pairs={{0,1},{3,2},{4,5},{7,6},{8,9},{11,10},{12,13},{15,14},{16,17},{19,... | collective-permute-start | bytes 1474568 | tf_op jit(solution)/shard_map/ppermute | solution.py:388
  35.2 8.7 %shard_map.72.refs_4_.refs_5_ = bf16[4,512,1024]{2,1,0:T(8,128)(2,1)} custom-call(bf16[1024,4096]{1,0:T(8,128)(2,1)} %w.1, bf16[272,1024]{1,0:T(8,128)(2,1)} %get-tuple-element.61.refs_0_, bf16[240,1024]{1,0:T(8,128)(2,1)} %get-tuple-element.62.refs_1_), custom_call_target="tpu_custom_call" | custom-call | flops 4294967296 | bytes 8388608 | tf_op jit(solution)/shard_map/pallas_call | solution.py:308
  43.9 1.4 %shard_map.73 = (bf16[272,1024]{1,0:T(8,128)(2,1)S(1)}, bf16[272,1024]{1,0:T(8,128)(2,1)S(1)}) custom-call(s32[1]{0:T(128)} %bitcast.3.refs_0_, s32[1]{0:T(128)} %bitcast.4.refs_1_, bf16[272,1024]{1,0:T(8,128)(2,1)S(1)} %collective-permute-done.5.refs_2_.refs_3_, bf16[272,1024]{1,0:T(8,128)(2,1)S(1)} %collective-permute-done.5.refs_2_.refs_3_, ...), custom_call_target="tpu_custom_call" | custom-call | flops 71303168 | bytes 278528 | tf_op jit(solution)/shard_map/pallas_call | solution.py:52
  45.3 4.1 %collective-permute-start.8 = (bf16[272,1024]{1,0:T(8,128)(2,1)S(1)}, bf16[272,1024]{1,0:T(8,128)(2,1)S(1)}, u32[]{:S(2)}, u32[]{:S(2)}) collective-permute-start(bf16[272,1024]{1,0:T(8,128)(2,1)S(1)} %get-tuple-element.63.refs_5_), channel_id=1, source_target_pairs={{0,1},{1,2},{4,5},{5,6},{8,9},{9,10},{12,13},{13,14},{16,17},{17,1... | collective-permute-start | bytes 1671176 | tf_op jit(solution)/shard_map/ppermute | solution.py:388
  50.2 4.0 %collective-permute-done.4.refs_2_.refs_3_ = bf16[240,1024]{1,0:T(8,128)(2,1)S(1)} collective-permute-done((bf16[240,1024]{1,0:T(8,128)(2,1)S(1)}, bf16[240,1024]{1,0:T(8,128)(2,1)S(1)}, u32[]{:S(2)}, u32[]{:S(2)}) %collective-permute-start.4) | collective-permute-done | bytes 491552 | tf_op jit(solution)/shard_map/ppermute | solution.py:388
  54.2 2.0 %shard_map.74 = (bf16[240,1024]{1,0:T(8,128)(2,1)}, bf16[240,1024]{1,0:T(8,128)(2,1)S(1)}) custom-call(s32[1]{0:T(128)} %bitcast.3.refs_0_, s32[1]{0:T(128)} %bitcast.4.refs_1_, bf16[240,1024]{1,0:T(8,128)(2,1)S(1)} %collective-permute-done.4.refs_2_.refs_3_, bf16[240,1024]{1,0:T(8,128)(2,1)S(1)} %collective-permute-done.4.refs_2_.refs_3_, ...), custom_call_target="tpu_custom_call" | custom-call | flops 62914560 | bytes 245760 | tf_op jit(solution)/shard_map/pallas_call | solution.py:52
  56.2 4.4 %collective-permute-start.6 = (bf16[240,1024]{1,0:T(8,128)(2,1)}, bf16[240,1024]{1,0:T(8,128)(2,1)S(1)}, u32[]{:S(2)}, u32[]{:S(2)}) collective-permute-start(bf16[240,1024]{1,0:T(8,128)(2,1)} %get-tuple-element.65.refs_6_), channel_id=1, source_target_pairs={{0,1},{1,2},{4,5},{5,6},{8,9},{9,10},{12,13},{13,14},{16,17},{17,1... | collective-permute-start | bytes 1474568 | tf_op jit(solution)/shard_map/ppermute | solution.py:388
  60.6 1.5 %collective-permute-start.7 = (bf16[240,1024]{1,0:T(8,128)(2,1)S(1)}, bf16[240,1024]{1,0:T(8,128)(2,1)}, u32[]{:S(2)}, u32[]{:S(2)}) collective-permute-start(bf16[240,1024]{1,0:T(8,128)(2,1)S(1)} %get-tuple-element.66.refs_7_), channel_id=1, source_target_pairs={{3,2},{2,1},{7,6},{6,5},{11,10},{10,9},{15,14},{14,13},{19,18},{18... | collective-permute-start | bytes 1474568 | tf_op jit(solution)/shard_map/ppermute | solution.py:388
  62.0 4.1 %collective-permute-done.8.refs_3_ = bf16[272,1024]{1,0:T(8,128)(2,1)S(1)} collective-permute-done((bf16[272,1024]{1,0:T(8,128)(2,1)S(1)}, bf16[272,1024]{1,0:T(8,128)(2,1)S(1)}, u32[]{:S(2)}, u32[]{:S(2)}) %collective-permute-start.8) | collective-permute-done | bytes 557088 | tf_op jit(solution)/shard_map/ppermute | solution.py:388
  66.1 1.4 %shard_map.75 = (bf16[272,1024]{1,0:T(8,128)(2,1)S(1)}, bf16[272,1024]{1,0:T(8,128)(2,1)S(1)}, bf16[272,1024]{1,0:T(8,128)(2,1)S(1)}) custom-call(s32[1]{0:T(128)} %bitcast.refs_0_, s32[1]{0:T(128)} %bitcast.1.refs_1_, s32[1]{0:T(128)} %bitcast.2.refs_2_, bf16[272,1024]{1,0:T(8,128)(2,1)S(1)} %collective-permute-done.8.refs_3_, ...), custom_call_target="tpu_custom_call" | custom-call | flops 71303168 | bytes 278528 | tf_op jit(solution)/shard_map/pallas_call | solution.py:52
  67.6 4.4 %collective-permute-start.12 = (bf16[272,1024]{1,0:T(8,128)(2,1)S(1)}, bf16[272,1024]{1,0:T(8,128)(2,1)S(1)}, u32[]{:S(2)}, u32[]{:S(2)}) collective-permute-start(bf16[272,1024]{1,0:T(8,128)(2,1)S(1)} %get-tuple-element.67.refs_6_), channel_id=1, source_target_pairs={{0,1},{1,2},{2,3},{4,5},{5,6},{6,7},{8,9},{9,10},{10,11},{12,13},{... | collective-permute-start | bytes 1671176 | tf_op jit(solution)/shard_map/ppermute | solution.py:388
  73.3 3.4 %collective-permute-done.6.refs_3_ = bf16[240,1024]{1,0:T(8,128)(2,1)S(1)} collective-permute-done((bf16[240,1024]{1,0:T(8,128)(2,1)}, bf16[240,1024]{1,0:T(8,128)(2,1)S(1)}, u32[]{:S(2)}, u32[]{:S(2)}) %collective-permute-start.6) | collective-permute-done | bytes 491552 | tf_op jit(solution)/shard_map/ppermute | solution.py:388
  76.8 2.4 %shard_map.76 = (bf16[240,1024]{1,0:T(8,128)(2,1)S(1)}, bf16[240,1024]{1,0:T(8,128)(2,1)S(1)}, bf16[240,1024]{1,0:T(8,128)(2,1)S(1)}) custom-call(s32[1]{0:T(128)} %bitcast.refs_0_, s32[1]{0:T(128)} %bitcast.1.refs_1_, s32[1]{0:T(128)} %bitcast.2.refs_2_, bf16[240,1024]{1,0:T(8,128)(2,1)S(1)} %collective-permute-done.6.refs_3_, ...), custom_call_target="tpu_custom_call" | custom-call | flops 62914560 | bytes 245760 | tf_op jit(solution)/shard_map/pallas_call | solution.py:52
  79.2 4.3 %collective-permute-start.10 = (bf16[240,1024]{1,0:T(8,128)(2,1)S(1)}, bf16[240,1024]{1,0:T(8,128)(2,1)S(1)}, u32[]{:S(2)}, u32[]{:S(2)}) collective-permute-start(bf16[240,1024]{1,0:T(8,128)(2,1)S(1)} %get-tuple-element.70), channel_id=1, source_target_pairs={{0,1},{1,2},{2,3},{4,5},{5,6},{6,7},{8,9},{9,10},{10,11},{12,13},{... | collective-permute-start | bytes 1474568 | tf_op jit(solution)/shard_map/ppermute | solution.py:388
  84.8 3.8 %collective-permute-done.12.up = bf16[272,1024]{1,0:T(8,128)(2,1)S(1)} collective-permute-done((bf16[272,1024]{1,0:T(8,128)(2,1)S(1)}, bf16[272,1024]{1,0:T(8,128)(2,1)S(1)}, u32[]{:S(2)}, u32[]{:S(2)}) %collective-permute-start.12) | collective-permute-done | bytes 557088 | tf_op jit(solution)/shard_map/ppermute | solution.py:388
  89.5 8.8 %collective-permute-done.10.up = bf16[240,1024]{1,0:T(8,128)(2,1)S(1)} collective-permute-done((bf16[240,1024]{1,0:T(8,128)(2,1)S(1)}, bf16[240,1024]{1,0:T(8,128)(2,1)S(1)}, u32[]{:S(2)}, u32[]{:S(2)}) %collective-permute-start.10) | collective-permute-done | bytes 491552 | tf_op jit(solution)/shard_map/ppermute | solution.py:388
  (21 shorter events, 10.2 us)
Async XLA Ops:
  8.4 15.2 %copy-start = (bf16[1024]{0:T(1024)(128)(2,1)S(1)}, bf16[1024]{0:T(1024)(128)(2,1)}, u32[]{:S(2)}) copy-start(bf16[1024]{0:T(1024)(128)(2,1)} %refs_2_.3) | copy-start | bytes 6148
  8.4 1.8 %collective-permute-start = (bf16[1296,128]{1,0:T(8,128)(2,1)S(1)}, bf16[1296,128]{1,0:T(8,128)(2,1)S(1)}, u32[]{:S(2)}, u32[]{:S(2)}) collective-permute-start(bf16[1296,128]{1,0:T(8,128)(2,1)S(1)} %get-tuple-element.39.mine), channel_id=1, source_target_pairs={{0,4},{4,0},{8,12},{12,8},{16,20},{20,16},{24,28},{28,24},{1,5},{5... | collective-permute-start | bytes 995336 | tf_op jit(solution)/shard_map/ppermute | solution.py:493
  10.3 6.3 %collective-permute-start.1 = (bf16[656,128]{1,0:T(8,128)(2,1)S(1)}, bf16[656,128]{1,0:T(8,128)(2,1)S(1)}, u32[]{:S(2)}, u32[]{:S(2)}) collective-permute-start(bf16[656,128]{1,0:T(8,128)(2,1)S(1)} %shard_map.65.mine), channel_id=1, source_target_pairs={{0,8},{4,20},{8,0},{12,28},{16,24},{20,4},{24,16},{28,12},{1,9},{5... | collective-permute-start | bytes 503816 | tf_op jit(solution)/shard_map/ppermute | solution.py:493
  16.6 5.5 %collective-permute-start.2 = (bf16[656,128]{1,0:T(8,128)(2,1)S(1)}, bf16[656,128]{1,0:T(8,128)(2,1)S(1)}, u32[]{:S(2)}, u32[]{:S(2)}) collective-permute-start(bf16[656,128]{1,0:T(8,128)(2,1)S(1)} %shard_map.66), channel_id=1, source_target_pairs={{0,16},{4,12},{8,24},{12,4},{16,0},{20,28},{24,8},{28,20},{1,17},{... | collective-permute-start | bytes 503816 | tf_op jit(solution)/shard_map/ppermute | solution.py:493
  22.2 1.5 %collective-permute-start.3 = (bf16[656,128]{1,0:T(8,128)(2,1)S(1)}, bf16[656,128]{1,0:T(8,128)(2,1)S(1)}, u32[]{:S(2)}, u32[]{:S(2)}) collective-permute-start(bf16[656,128]{1,0:T(8,128)(2,1)S(1)} %shard_map.69.refs_4_), channel_id=1, source_target_pairs={{0,4},{4,0},{8,12},{12,8},{16,20},{20,16},{24,28},{28,24},{1,5},{5... | collective-permute-start | bytes 503816 | tf_op jit(solution)/shard_map/ppermute | solution.py:493
  26.7 17.3 %collective-permute-start.5 = (bf16[272,1024]{1,0:T(8,128)(2,1)S(1)}, bf16[272,1024]{1,0:T(8,128)(2,1)S(1)}, u32[]{:S(2)}, u32[]{:S(2)}) collective-permute-start(bf16[272,1024]{1,0:T(8,128)(2,1)S(1)} %get-tuple-element.59.refs_11_), channel_id=1, source_target_pairs={{0,1},{3,2},{4,5},{7,6},{8,9},{11,10},{12,13},{15,14},{16,17},{19,... | collective-permute-start | bytes 1671176 | tf_op jit(solution)/shard_map/ppermute | solution.py:388
  33.7 20.5 %collective-permute-start.4 = (bf16[240,1024]{1,0:T(8,128)(2,1)S(1)}, bf16[240,1024]{1,0:T(8,128)(2,1)S(1)}, u32[]{:S(2)}, u32[]{:S(2)}) collective-permute-start(bf16[240,1024]{1,0:T(8,128)(2,1)S(1)} %get-tuple-element.60), channel_id=1, source_target_pairs={{0,1},{3,2},{4,5},{7,6},{8,9},{11,10},{12,13},{15,14},{16,17},{19,... | collective-permute-start | bytes 1474568 | tf_op jit(solution)/shard_map/ppermute | solution.py:388
  45.3 20.8 %collective-permute-start.8 = (bf16[272,1024]{1,0:T(8,128)(2,1)S(1)}, bf16[272,1024]{1,0:T(8,128)(2,1)S(1)}, u32[]{:S(2)}, u32[]{:S(2)}) collective-permute-start(bf16[272,1024]{1,0:T(8,128)(2,1)S(1)} %get-tuple-element.63.refs_5_), channel_id=1, source_target_pairs={{0,1},{1,2},{4,5},{5,6},{8,9},{9,10},{12,13},{13,14},{16,17},{17,1... | collective-permute-start | bytes 1671176 | tf_op jit(solution)/shard_map/ppermute | solution.py:388
  49.5 16.7 %collective-permute-start.9 = (bf16[272,1024]{1,0:T(8,128)(2,1)S(1)}, bf16[272,1024]{1,0:T(8,128)(2,1)S(1)}, u32[]{:S(2)}, u32[]{:S(2)}) collective-permute-start(bf16[272,1024]{1,0:T(8,128)(2,1)S(1)} %get-tuple-element.64.refs_6_), channel_id=1, source_target_pairs={{3,2},{2,1},{7,6},{6,5},{11,10},{10,9},{15,14},{14,13},{19,18},{18... | collective-permute-start | bytes 1671176 | tf_op jit(solution)/shard_map/ppermute | solution.py:388
  56.2 20.6 %collective-permute-start.6 = (bf16[240,1024]{1,0:T(8,128)(2,1)}, bf16[240,1024]{1,0:T(8,128)(2,1)S(1)}, u32[]{:S(2)}, u32[]{:S(2)}) collective-permute-start(bf16[240,1024]{1,0:T(8,128)(2,1)} %get-tuple-element.65.refs_6_), channel_id=1, source_target_pairs={{0,1},{1,2},{4,5},{5,6},{8,9},{9,10},{12,13},{13,14},{16,17},{17,1... | collective-permute-start | bytes 1474568 | tf_op jit(solution)/shard_map/ppermute | solution.py:388
  60.6 16.2 %collective-permute-start.7 = (bf16[240,1024]{1,0:T(8,128)(2,1)S(1)}, bf16[240,1024]{1,0:T(8,128)(2,1)}, u32[]{:S(2)}, u32[]{:S(2)}) collective-permute-start(bf16[240,1024]{1,0:T(8,128)(2,1)S(1)} %get-tuple-element.66.refs_7_), channel_id=1, source_target_pairs={{3,2},{2,1},{7,6},{6,5},{11,10},{10,9},{15,14},{14,13},{19,18},{18... | collective-permute-start | bytes 1474568 | tf_op jit(solution)/shard_map/ppermute | solution.py:388
  67.6 21.0 %collective-permute-start.12 = (bf16[272,1024]{1,0:T(8,128)(2,1)S(1)}, bf16[272,1024]{1,0:T(8,128)(2,1)S(1)}, u32[]{:S(2)}, u32[]{:S(2)}) collective-permute-start(bf16[272,1024]{1,0:T(8,128)(2,1)S(1)} %get-tuple-element.67.refs_6_), channel_id=1, source_target_pairs={{0,1},{1,2},{2,3},{4,5},{5,6},{6,7},{8,9},{9,10},{10,11},{12,13},{... | collective-permute-start | bytes 1671176 | tf_op jit(solution)/shard_map/ppermute | solution.py:388
  72.0 16.6 %collective-permute-start.13 = (bf16[272,1024]{1,0:T(8,128)(2,1)S(1)}, bf16[272,1024]{1,0:T(8,128)(2,1)S(1)}, u32[]{:S(2)}, u32[]{:S(2)}) collective-permute-start(bf16[272,1024]{1,0:T(8,128)(2,1)S(1)} %get-tuple-element.68.refs_7_), channel_id=1, source_target_pairs={{3,2},{2,1},{1,0},{7,6},{6,5},{5,4},{11,10},{10,9},{9,8},{15,14},{... | collective-permute-start | bytes 1671176 | tf_op jit(solution)/shard_map/ppermute | solution.py:388
  79.2 19.1 %collective-permute-start.10 = (bf16[240,1024]{1,0:T(8,128)(2,1)S(1)}, bf16[240,1024]{1,0:T(8,128)(2,1)S(1)}, u32[]{:S(2)}, u32[]{:S(2)}) collective-permute-start(bf16[240,1024]{1,0:T(8,128)(2,1)S(1)} %get-tuple-element.70), channel_id=1, source_target_pairs={{0,1},{1,2},{2,3},{4,5},{5,6},{6,7},{8,9},{9,10},{10,11},{12,13},{... | collective-permute-start | bytes 1474568 | tf_op jit(solution)/shard_map/ppermute | solution.py:388
  83.5 14.8 %collective-permute-start.11 = (bf16[240,1024]{1,0:T(8,128)(2,1)S(1)}, bf16[240,1024]{1,0:T(8,128)(2,1)S(1)}, u32[]{:S(2)}, u32[]{:S(2)}) collective-permute-start(bf16[240,1024]{1,0:T(8,128)(2,1)S(1)} %get-tuple-element.71), channel_id=1, source_target_pairs={{3,2},{2,1},{1,0},{7,6},{6,5},{5,4},{11,10},{10,9},{9,8},{15,14},{... | collective-permute-start | bytes 1474568 | tf_op jit(solution)/shard_map/ppermute | solution.py:388

commit v4 on v2

--- a/solution.py
+++ b/solution.py
@@ -14,7 +14,7 @@
 WIDE = 256
 HALF_ROOT = 0.7071067811865476
 DEPTH_TILE = 1024
-AHEAD = 3
+AHEAD = 4
 PIECES = 2
 VMEM_LIMIT = 24 * 1024 * 1024
 NT = (((1,), (1,)), ((), ()))

time: 100 us -> 100 us (level)
  no operation moved by 1% of the time
where the time goes in v4:
time: 100 us; the launch traced here: 99.4 us
  Pallas kernels  37.6 us (38%)
  starting transfers between devices  32.3 us (32%)
  waiting for transfers between devices  29.1 us (29%)
    pallas_call x14, Pallas kernels, call(): pl.pallas_call(kernel, in_specs=[pl.BlockSpec(memory_space=pltpu.SMEM)] *...  28.9 us
    ppermute x10, starting transfers between devices, send(): return lax.ppermute(block, 'tp', pairs)  26.7 us
    ppermute x10, waiting for transfers between devices, send(): return lax.ppermute(block, 'tp', pairs)  24.8 us
    pallas_call x1, Pallas kernels, partials(): pl.pallas_call(partials_kernel, grid=(count,), in_specs=[pl.BlockSpec((de...  8.76 us
    ppermute x4, starting transfers between devices, swap(): lax.ppermute(block, 'ctx', [(i, i ^ 1 << across[i]) for i in range(shards)])  5.63 us
    ppermute x4, waiting for transfers between devices, swap(): lax.ppermute(block, 'ctx', [(i, i ^ 1 << across[i]) for i in range(shards)])  4.27 us
  transfers between devices with their start and end apart: 14, of which 9 were waited for; matrix products, arithmetic and copies ran while one was open for 0% of the time, Pallas kernels for 25%

profile of v4, /device:TPU:0, one launch (start us, length us, event | category | flops | bytes accessed | tf_op | source)
XLA Modules:
  0.0 99.4 jit_solution(5475597451210343206)
XLA Ops:
  0.0 8.4 %shard_map.64 = (bf16[512,128]{1,0:T(8,128)(2,1)S(1)}, bf16[512,128]{1,0:T(8,128)(2,1)S(1)}, bf16[512,1024]{1,0:T(8,128)(2,1)S(1)}, bf16[1296,128]{1,0:T(8,128)(2,1)S(1)}) custom-call(bf16[512,4096]{1,0:T(8,128)(2,1)} %tokens.1, bf16[4096,128]{1,0:T(8,128)(2,1)} %wq.1, bf16[4096,128]{1,0:T(8,128)(2,1)} %wk.1, bf16[4096,1024]{1,0:T(8,128)(2,1)} %wv.1), custom_call_target="tpu_custom_call" | custom-call | flops 5368709120 | bytes 20971520 | tf_op jit(solution)/shard_map/pallas_call | solution.py:52
  10.3 2.9 %collective-permute-start.1 = (bf16[656,128]{1,0:T(8,128)(2,1)S(1)}, bf16[656,128]{1,0:T(8,128)(2,1)S(1)}, u32[]{:S(2)}, u32[]{:S(2)}) collective-permute-start(bf16[656,128]{1,0:T(8,128)(2,1)S(1)} %shard_map.65.mine), channel_id=1, source_target_pairs={{0,8},{4,20},{8,0},{12,28},{16,24},{20,4},{24,16},{28,12},{1,9},{5... | collective-permute-start | bytes 503816 | tf_op jit(solution)/shard_map/ppermute | solution.py:491
  13.2 2.5 %shard_map.67 = (bf16[512,512]{1,0:T(8,128)(2,1)}, bf16[4,512,256]{2,1,0:T(8,128)(2,1)}) custom-call(bf16[512,128]{1,0:T(8,128)(2,1)S(1)} %get-tuple-element.48.q, bf16[512,128]{1,0:T(8,128)(2,1)S(1)} %get-tuple-element.49.k, bf16[512,1024]{1,0:T(8,128)(2,1)S(1)} %get-tuple-element.50.v), custom_call_target="tpu_custom_call" | custom-call | flops 1073741824 | bytes 4194304 | tf_op jit(solution)/shard_map/pallas_call | solution.py:52
  16.6 2.1 %collective-permute-start.2 = (bf16[656,128]{1,0:T(8,128)(2,1)S(1)}, bf16[656,128]{1,0:T(8,128)(2,1)S(1)}, u32[]{:S(2)}, u32[]{:S(2)}) collective-permute-start(bf16[656,128]{1,0:T(8,128)(2,1)S(1)} %shard_map.66), channel_id=1, source_target_pairs={{0,16},{4,12},{8,24},{12,4},{16,0},{20,28},{24,8},{28,20},{1,17},{... | collective-permute-start | bytes 503816 | tf_op jit(solution)/shard_map/ppermute | solution.py:491
  18.8 2.5 %shard_map.68 = (bf16[512,512]{1,0:T(8,128)(2,1)}, bf16[4,512,256]{2,1,0:T(8,128)(2,1)}) custom-call(bf16[512,128]{1,0:T(8,128)(2,1)S(1)} %get-tuple-element.48.q, bf16[512,128]{1,0:T(8,128)(2,1)S(1)} %get-tuple-element.49.k, bf16[512,1024]{1,0:T(8,128)(2,1)S(1)} %get-tuple-element.50.v), custom_call_target="tpu_custom_call" | custom-call | flops 1073741824 | bytes 4194304 | tf_op jit(solution)/shard_map/pallas_call | solution.py:52
  22.3 1.4 %collective-permute-done.3.refs_5_ = bf16[656,128]{1,0:T(8,128)(2,1)S(1)} collective-permute-done((bf16[656,128]{1,0:T(8,128)(2,1)S(1)}, bf16[656,128]{1,0:T(8,128)(2,1)S(1)}, u32[]{:S(2)}, u32[]{:S(2)}) %collective-permute-start.3) | collective-permute-done | bytes 167968 | tf_op jit(solution)/shard_map/ppermute | solution.py:491
  23.6 3.1 %shard_map.70 = (bf16[256,1024]{1,0:T(8,128)(2,1)}, bf16[256,1024]{1,0:T(8,128)(2,1)S(1)}) custom-call(s32[1]{0:T(128)} %bitcast.5.me.refs_0_, s32[1]{0:T(128)} %bitcast.6.refs_1_, bf16[1024]{0:T(1024)(128)(2,1)S(1)} %copy-done, bf16[1296,128]{1,0:T(8,128)(2,1)S(1)} %collective-permute-done.other.refs_3_, bf16[656,128]{1,0:T(8,128)(2,1)S(1)} %shard_map.69.refs_4_, ...), custom_call_target="tpu_custom_call" | custom-call | flops 805306368 | bytes 3145728 | tf_op jit(solution)/shard_map/pallas_call | solution.py:52
  26.7 4.0 %collective-permute-start.5 = (bf16[256,1024]{1,0:T(8,128)(2,1)S(1)}, bf16[256,1024]{1,0:T(8,128)(2,1)S(1)}, u32[]{:S(2)}, u32[]{:S(2)}) collective-permute-start(bf16[256,1024]{1,0:T(8,128)(2,1)S(1)} %get-tuple-element.59.refs_11_), channel_id=1, source_target_pairs={{0,1},{3,2},{4,5},{7,6},{8,9},{11,10},{12,13},{15,14},{16,17},{19,... | collective-permute-start | bytes 1572872 | tf_op jit(solution)/shard_map/ppermute | solution.py:386
  30.7 3.0 %shard_map.71 = (bf16[256,1024]{1,0:T(8,128)(2,1)}, bf16[256,1024]{1,0:T(8,128)(2,1)S(1)}) custom-call(s32[1]{0:T(128)} %bitcast.5.me.refs_0_, s32[1]{0:T(128)} %bitcast.6.refs_1_, bf16[1024]{0:T(1024)(128)(2,1)S(1)} %copy-done, bf16[1296,128]{1,0:T(8,128)(2,1)S(1)} %collective-permute-done.other.refs_3_, bf16[656,128]{1,0:T(8,128)(2,1)S(1)} %shard_map.69.refs_4_, ...), custom_call_target="tpu_custom_call" | custom-call | flops 805306368 | bytes 3145728 | tf_op jit(solution)/shard_map/pallas_call | solution.py:52
  33.8 1.5 %collective-permute-start.4 = (bf16[256,1024]{1,0:T(8,128)(2,1)S(1)}, bf16[256,1024]{1,0:T(8,128)(2,1)S(1)}, u32[]{:S(2)}, u32[]{:S(2)}) collective-permute-start(bf16[256,1024]{1,0:T(8,128)(2,1)S(1)} %get-tuple-element.60), channel_id=1, source_target_pairs={{0,1},{3,2},{4,5},{7,6},{8,9},{11,10},{12,13},{15,14},{16,17},{19,... | collective-permute-start | bytes 1572872 | tf_op jit(solution)/shard_map/ppermute | solution.py:386
  35.3 8.8 %shard_map.72.refs_4_.refs_5_ = bf16[4,512,1024]{2,1,0:T(8,128)(2,1)} custom-call(bf16[1024,4096]{1,0:T(8,128)(2,1)} %w.1, bf16[256,1024]{1,0:T(8,128)(2,1)} %get-tuple-element.61.refs_0_, bf16[256,1024]{1,0:T(8,128)(2,1)} %get-tuple-element.62.refs_1_), custom_call_target="tpu_custom_call" | custom-call | flops 4294967296 | bytes 8388608 | tf_op jit(solution)/shard_map/pallas_call | solution.py:306
  44.1 2.0 %shard_map.73 = (bf16[256,1024]{1,0:T(8,128)(2,1)}, bf16[256,1024]{1,0:T(8,128)(2,1)S(1)}) custom-call(s32[1]{0:T(128)} %bitcast.3.refs_0_, s32[1]{0:T(128)} %bitcast.4.refs_1_, bf16[256,1024]{1,0:T(8,128)(2,1)S(1)} %collective-permute-done.5.refs_2_.refs_3_, bf16[256,1024]{1,0:T(8,128)(2,1)S(1)} %collective-permute-done.5.refs_2_.refs_3_, ...), custom_call_target="tpu_custom_call" | custom-call | flops 67108864 | bytes 262144 | tf_op jit(solution)/shard_map/pallas_call | solution.py:52
  46.1 3.3 %collective-permute-start.8 = (bf16[256,1024]{1,0:T(8,128)(2,1)}, bf16[256,1024]{1,0:T(8,128)(2,1)S(1)}, u32[]{:S(2)}, u32[]{:S(2)}) collective-permute-start(bf16[256,1024]{1,0:T(8,128)(2,1)} %get-tuple-element.63.refs_5_), channel_id=1, source_target_pairs={{0,1},{1,2},{4,5},{5,6},{8,9},{9,10},{12,13},{13,14},{16,17},{17,1... | collective-permute-start | bytes 1572872 | tf_op jit(solution)/shard_map/ppermute | solution.py:386
  49.4 1.5 %collective-permute-start.9 = (bf16[256,1024]{1,0:T(8,128)(2,1)S(1)}, bf16[256,1024]{1,0:T(8,128)(2,1)}, u32[]{:S(2)}, u32[]{:S(2)}) collective-permute-start(bf16[256,1024]{1,0:T(8,128)(2,1)S(1)} %get-tuple-element.64.refs_6_), channel_id=1, source_target_pairs={{3,2},{2,1},{7,6},{6,5},{11,10},{10,9},{15,14},{14,13},{19,18},{18... | collective-permute-start | bytes 1572872 | tf_op jit(solution)/shard_map/ppermute | solution.py:386
  50.9 3.3 %collective-permute-done.4.refs_2_.refs_3_ = bf16[256,1024]{1,0:T(8,128)(2,1)S(1)} collective-permute-done((bf16[256,1024]{1,0:T(8,128)(2,1)S(1)}, bf16[256,1024]{1,0:T(8,128)(2,1)S(1)}, u32[]{:S(2)}, u32[]{:S(2)}) %collective-permute-start.4) | collective-permute-done | bytes 524320 | tf_op jit(solution)/shard_map/ppermute | solution.py:386
  55.5 4.4 %collective-permute-start.6 = (bf16[256,1024]{1,0:T(8,128)(2,1)S(1)}, bf16[256,1024]{1,0:T(8,128)(2,1)S(1)}, u32[]{:S(2)}, u32[]{:S(2)}) collective-permute-start(bf16[256,1024]{1,0:T(8,128)(2,1)S(1)} %get-tuple-element.65.refs_6_), channel_id=1, source_target_pairs={{0,1},{1,2},{4,5},{5,6},{8,9},{9,10},{12,13},{13,14},{16,17},{17,1... | collective-permute-start | bytes 1572872 | tf_op jit(solution)/shard_map/ppermute | solution.py:386
  60.7 4.9 %collective-permute-done.8.refs_3_ = bf16[256,1024]{1,0:T(8,128)(2,1)S(1)} collective-permute-done((bf16[256,1024]{1,0:T(8,128)(2,1)}, bf16[256,1024]{1,0:T(8,128)(2,1)S(1)}, u32[]{:S(2)}, u32[]{:S(2)}) %collective-permute-start.8) | collective-permute-done | bytes 524320 | tf_op jit(solution)/shard_map/ppermute | solution.py:386
  65.5 2.5 %shard_map.75 = (bf16[256,1024]{1,0:T(8,128)(2,1)S(1)}, bf16[256,1024]{1,0:T(8,128)(2,1)S(1)}, bf16[256,1024]{1,0:T(8,128)(2,1)S(1)}) custom-call(s32[1]{0:T(128)} %bitcast.refs_0_, s32[1]{0:T(128)} %bitcast.1.refs_1_, s32[1]{0:T(128)} %bitcast.2.refs_2_, bf16[256,1024]{1,0:T(8,128)(2,1)S(1)} %collective-permute-done.8.refs_3_, ...), custom_call_target="tpu_custom_call" | custom-call | flops 67108864 | bytes 262144 | tf_op jit(solution)/shard_map/pallas_call | solution.py:52
  68.0 4.3 %collective-permute-start.12 = (bf16[256,1024]{1,0:T(8,128)(2,1)S(1)}, bf16[256,1024]{1,0:T(8,128)(2,1)S(1)}, u32[]{:S(2)}, u32[]{:S(2)}) collective-permute-start(bf16[256,1024]{1,0:T(8,128)(2,1)S(1)} %get-tuple-element.67.refs_6_), channel_id=1, source_target_pairs={{0,1},{1,2},{2,3},{4,5},{5,6},{6,7},{8,9},{9,10},{10,11},{12,13},{... | collective-permute-start | bytes 1572872 | tf_op jit(solution)/shard_map/ppermute | solution.py:386
  73.6 3.0 %collective-permute-done.6.refs_3_ = bf16[256,1024]{1,0:T(8,128)(2,1)S(1)} collective-permute-done((bf16[256,1024]{1,0:T(8,128)(2,1)S(1)}, bf16[256,1024]{1,0:T(8,128)(2,1)S(1)}, u32[]{:S(2)}, u32[]{:S(2)}) %collective-permute-start.6) | collective-permute-done | bytes 524320 | tf_op jit(solution)/shard_map/ppermute | solution.py:386
  76.7 1.4 %shard_map.76 = (bf16[256,1024]{1,0:T(8,128)(2,1)S(1)}, bf16[256,1024]{1,0:T(8,128)(2,1)S(1)}, bf16[256,1024]{1,0:T(8,128)(2,1)S(1)}) custom-call(s32[1]{0:T(128)} %bitcast.refs_0_, s32[1]{0:T(128)} %bitcast.1.refs_1_, s32[1]{0:T(128)} %bitcast.2.refs_2_, bf16[256,1024]{1,0:T(8,128)(2,1)S(1)} %collective-permute-done.6.refs_3_, ...), custom_call_target="tpu_custom_call" | custom-call | flops 67108864 | bytes 262144 | tf_op jit(solution)/shard_map/pallas_call | solution.py:52
  78.1 4.4 %collective-permute-start.10 = (bf16[256,1024]{1,0:T(8,128)(2,1)S(1)}, bf16[256,1024]{1,0:T(8,128)(2,1)S(1)}, u32[]{:S(2)}, u32[]{:S(2)}) collective-permute-start(bf16[256,1024]{1,0:T(8,128)(2,1)S(1)} %get-tuple-element.70), channel_id=1, source_target_pairs={{0,1},{1,2},{2,3},{4,5},{5,6},{6,7},{8,9},{9,10},{10,11},{12,13},{... | collective-permute-start | bytes 1572872 | tf_op jit(solution)/shard_map/ppermute | solution.py:386
  83.8 4.1 %collective-permute-done.12.up = bf16[256,1024]{1,0:T(8,128)(2,1)S(1)} collective-permute-done((bf16[256,1024]{1,0:T(8,128)(2,1)S(1)}, bf16[256,1024]{1,0:T(8,128)(2,1)S(1)}, u32[]{:S(2)}, u32[]{:S(2)}) %collective-permute-start.12) | collective-permute-done | bytes 524320 | tf_op jit(solution)/shard_map/ppermute | solution.py:386
  88.8 9.5 %collective-permute-done.10.up = bf16[256,1024]{1,0:T(8,128)(2,1)S(1)} collective-permute-done((bf16[256,1024]{1,0:T(8,128)(2,1)S(1)}, bf16[256,1024]{1,0:T(8,128)(2,1)S(1)}, u32[]{:S(2)}, u32[]{:S(2)}) %collective-permute-start.10) | collective-permute-done | bytes 524320 | tf_op jit(solution)/shard_map/ppermute | solution.py:386
  (21 shorter events, 10.2 us)
Async XLA Ops:
  8.4 15.2 %copy-start = (bf16[1024]{0:T(1024)(128)(2,1)S(1)}, bf16[1024]{0:T(1024)(128)(2,1)}, u32[]{:S(2)}) copy-start(bf16[1024]{0:T(1024)(128)(2,1)} %refs_2_.3) | copy-start | bytes 6148
  8.4 1.8 %collective-permute-start = (bf16[1296,128]{1,0:T(8,128)(2,1)S(1)}, bf16[1296,128]{1,0:T(8,128)(2,1)S(1)}, u32[]{:S(2)}, u32[]{:S(2)}) collective-permute-start(bf16[1296,128]{1,0:T(8,128)(2,1)S(1)} %get-tuple-element.39.mine), channel_id=1, source_target_pairs={{0,4},{4,0},{8,12},{12,8},{16,20},{20,16},{24,28},{28,24},{1,5},{5... | collective-permute-start | bytes 995336 | tf_op jit(solution)/shard_map/ppermute | solution.py:491
  10.3 6.3 %collective-permute-start.1 = (bf16[656,128]{1,0:T(8,128)(2,1)S(1)}, bf16[656,128]{1,0:T(8,128)(2,1)S(1)}, u32[]{:S(2)}, u32[]{:S(2)}) collective-permute-start(bf16[656,128]{1,0:T(8,128)(2,1)S(1)} %shard_map.65.mine), channel_id=1, source_target_pairs={{0,8},{4,20},{8,0},{12,28},{16,24},{20,4},{24,16},{28,12},{1,9},{5... | collective-permute-start | bytes 503816 | tf_op jit(solution)/shard_map/ppermute | solution.py:491
  16.6 5.5 %collective-permute-start.2 = (bf16[656,128]{1,0:T(8,128)(2,1)S(1)}, bf16[656,128]{1,0:T(8,128)(2,1)S(1)}, u32[]{:S(2)}, u32[]{:S(2)}) collective-permute-start(bf16[656,128]{1,0:T(8,128)(2,1)S(1)} %shard_map.66), channel_id=1, source_target_pairs={{0,16},{4,12},{8,24},{12,4},{16,0},{20,28},{24,8},{28,20},{1,17},{... | collective-permute-start | bytes 503816 | tf_op jit(solution)/shard_map/ppermute | solution.py:491
  22.2 1.5 %collective-permute-start.3 = (bf16[656,128]{1,0:T(8,128)(2,1)S(1)}, bf16[656,128]{1,0:T(8,128)(2,1)S(1)}, u32[]{:S(2)}, u32[]{:S(2)}) collective-permute-start(bf16[656,128]{1,0:T(8,128)(2,1)S(1)} %shard_map.69.refs_4_), channel_id=1, source_target_pairs={{0,4},{4,0},{8,12},{12,8},{16,20},{20,16},{24,28},{28,24},{1,5},{5... | collective-permute-start | bytes 503816 | tf_op jit(solution)/shard_map/ppermute | solution.py:491
  26.7 17.4 %collective-permute-start.5 = (bf16[256,1024]{1,0:T(8,128)(2,1)S(1)}, bf16[256,1024]{1,0:T(8,128)(2,1)S(1)}, u32[]{:S(2)}, u32[]{:S(2)}) collective-permute-start(bf16[256,1024]{1,0:T(8,128)(2,1)S(1)} %get-tuple-element.59.refs_11_), channel_id=1, source_target_pairs={{0,1},{3,2},{4,5},{7,6},{8,9},{11,10},{12,13},{15,14},{16,17},{19,... | collective-permute-start | bytes 1572872 | tf_op jit(solution)/shard_map/ppermute | solution.py:386
  33.8 20.4 %collective-permute-start.4 = (bf16[256,1024]{1,0:T(8,128)(2,1)S(1)}, bf16[256,1024]{1,0:T(8,128)(2,1)S(1)}, u32[]{:S(2)}, u32[]{:S(2)}) collective-permute-start(bf16[256,1024]{1,0:T(8,128)(2,1)S(1)} %get-tuple-element.60), channel_id=1, source_target_pairs={{0,1},{3,2},{4,5},{7,6},{8,9},{11,10},{12,13},{15,14},{16,17},{19,... | collective-permute-start | bytes 1572872 | tf_op jit(solution)/shard_map/ppermute | solution.py:386
  46.1 19.4 %collective-permute-start.8 = (bf16[256,1024]{1,0:T(8,128)(2,1)}, bf16[256,1024]{1,0:T(8,128)(2,1)S(1)}, u32[]{:S(2)}, u32[]{:S(2)}) collective-permute-start(bf16[256,1024]{1,0:T(8,128)(2,1)} %get-tuple-element.63.refs_5_), channel_id=1, source_target_pairs={{0,1},{1,2},{4,5},{5,6},{8,9},{9,10},{12,13},{13,14},{16,17},{17,1... | collective-permute-start | bytes 1572872 | tf_op jit(solution)/shard_map/ppermute | solution.py:386
  49.4 16.1 %collective-permute-start.9 = (bf16[256,1024]{1,0:T(8,128)(2,1)S(1)}, bf16[256,1024]{1,0:T(8,128)(2,1)}, u32[]{:S(2)}, u32[]{:S(2)}) collective-permute-start(bf16[256,1024]{1,0:T(8,128)(2,1)S(1)} %get-tuple-element.64.refs_6_), channel_id=1, source_target_pairs={{3,2},{2,1},{7,6},{6,5},{11,10},{10,9},{15,14},{14,13},{19,18},{18... | collective-permute-start | bytes 1572872 | tf_op jit(solution)/shard_map/ppermute | solution.py:386
  55.5 21.1 %collective-permute-start.6 = (bf16[256,1024]{1,0:T(8,128)(2,1)S(1)}, bf16[256,1024]{1,0:T(8,128)(2,1)S(1)}, u32[]{:S(2)}, u32[]{:S(2)}) collective-permute-start(bf16[256,1024]{1,0:T(8,128)(2,1)S(1)} %get-tuple-element.65.refs_6_), channel_id=1, source_target_pairs={{0,1},{1,2},{4,5},{5,6},{8,9},{9,10},{12,13},{13,14},{16,17},{17,1... | collective-permute-start | bytes 1572872 | tf_op jit(solution)/shard_map/ppermute | solution.py:386
  60.0 16.7 %collective-permute-start.7 = (bf16[256,1024]{1,0:T(8,128)(2,1)S(1)}, bf16[256,1024]{1,0:T(8,128)(2,1)S(1)}, u32[]{:S(2)}, u32[]{:S(2)}) collective-permute-start(bf16[256,1024]{1,0:T(8,128)(2,1)S(1)} %get-tuple-element.66.refs_7_), channel_id=1, source_target_pairs={{3,2},{2,1},{7,6},{6,5},{11,10},{10,9},{15,14},{14,13},{19,18},{18... | collective-permute-start | bytes 1572872 | tf_op jit(solution)/shard_map/ppermute | solution.py:386
  68.0 19.9 %collective-permute-start.12 = (bf16[256,1024]{1,0:T(8,128)(2,1)S(1)}, bf16[256,1024]{1,0:T(8,128)(2,1)S(1)}, u32[]{:S(2)}, u32[]{:S(2)}) collective-permute-start(bf16[256,1024]{1,0:T(8,128)(2,1)S(1)} %get-tuple-element.67.refs_6_), channel_id=1, source_target_pairs={{0,1},{1,2},{2,3},{4,5},{5,6},{6,7},{8,9},{9,10},{10,11},{12,13},{... | collective-permute-start | bytes 1572872 | tf_op jit(solution)/shard_map/ppermute | solution.py:386
  72.3 15.6 %collective-permute-start.13 = (bf16[256,1024]{1,0:T(8,128)(2,1)S(1)}, bf16[256,1024]{1,0:T(8,128)(2,1)S(1)}, u32[]{:S(2)}, u32[]{:S(2)}) collective-permute-start(bf16[256,1024]{1,0:T(8,128)(2,1)S(1)} %get-tuple-element.68.refs_7_), channel_id=1, source_target_pairs={{3,2},{2,1},{1,0},{7,6},{6,5},{5,4},{11,10},{10,9},{9,8},{15,14},{... | collective-permute-start | bytes 1572872 | tf_op jit(solution)/shard_map/ppermute | solution.py:386
  78.1 20.2 %collective-permute-start.10 = (bf16[256,1024]{1,0:T(8,128)(2,1)S(1)}, bf16[256,1024]{1,0:T(8,128)(2,1)S(1)}, u32[]{:S(2)}, u32[]{:S(2)}) collective-permute-start(bf16[256,1024]{1,0:T(8,128)(2,1)S(1)} %get-tuple-element.70), channel_id=1, source_target_pairs={{0,1},{1,2},{2,3},{4,5},{5,6},{6,7},{8,9},{9,10},{10,11},{12,13},{... | collective-permute-start | bytes 1572872 | tf_op jit(solution)/shard_map/ppermute | solution.py:386
  82.5 15.8 %collective-permute-start.11 = (bf16[256,1024]{1,0:T(8,128)(2,1)S(1)}, bf16[256,1024]{1,0:T(8,128)(2,1)S(1)}, u32[]{:S(2)}, u32[]{:S(2)}) collective-permute-start(bf16[256,1024]{1,0:T(8,128)(2,1)S(1)} %get-tuple-element.71), channel_id=1, source_target_pairs={{3,2},{2,1},{1,0},{7,6},{6,5},{5,4},{11,10},{10,9},{9,8},{15,14},{... | collective-permute-start | bytes 1572872 | tf_op jit(solution)/shard_map/ppermute | solution.py:386
